TPU v7x, 256 devices: a whole 4x4x8 slice. The times are simulated.
256 devices in a mesh: seq: 2 (over core), expert: 16 (over x, y), tensor: 8 (over z).
Axes of the slice: x: 4, y: 4, z: 8, core: 2. Of those that a mesh axis runs over, the one named last changes fastest.
Arguments:
- tokens: bfloat16 [2048, 6400], P('expert', ('seq', 'tensor')), may hold values from -6 to 6
- expert_ids: int32 [2048], P('expert'), may hold values from 0 to 15, as said below
- gate_weights: float32 [2048], P('expert'), may hold values from 0.3 to 1
- gate_up_codes: float32 [16, 2, 1280, 10240], P('expert', None, None, ('seq', 'tensor')), may hold values from 0 to 1048575, as said below
- gate_up_scales: float32 [16, 2, 50, 10240], P('expert', None, None, ('seq', 'tensor')), may hold values from 0.001375 to 0.0055
- down_codes: float32 [16, 2048, 6400], P('expert', ('seq', 'tensor')), may hold values from 0 to 1048575, as said below
- down_scales: float32 [16, 80, 6400], P('expert', ('seq', 'tensor')), may hold values from 0.001087033 to 0.004348132
- shared_gate_up_codes: float32 [2, 1280, 10240], P(None, 'expert', ('seq', 'tensor')), may hold values from 0 to 1048575, as said below
- shared_gate_up_scales: float32 [2, 50, 10240], P(None, None, ('seq', 'tensor')), may hold values from 0.001375 to 0.0055
- shared_down_codes: float32 [2048, 6400], P(('seq', 'tensor'), 'expert'), may hold values from 0 to 1048575, as said below
- shared_down_scales: float32 [80, 6400], P(('seq', 'tensor')), may hold values from 0.001087033 to 0.004348132
Outputs:
- mixed: bfloat16 [2048, 6400], P('expert', ('seq', 'tensor'))
Inputs may be any that keep to these rules, and one draw needn't show every extreme that they name: `expert_ids`: among the 128 tokens of each aligned block no expert is named more than 16 times; in every draw one expert is named exactly 16 times in every block. `gate_up_codes`: every entry is a whole number; its five base-16 digits are the codes. `down_codes`: every entry is a whole number; its five base-16 digits are the codes. `shared_gate_up_codes`: every entry is a whole number; its five base-16 digits are the codes. `shared_down_codes`: every entry is a whole number; its five base-16 digits are the codes.
All inputs are finite; a program needn't handle non-finite values.
Results may differ from a plain program's by a relative error of at most 0.022.
Values may be sent and summed in bfloat16 or wider, within the bound.
A program may use at most 192 MiB of HBM per device.

v0:
```python
import functools

import jax
import jax.numpy as jnp
from jax import lax
from jax.experimental import pallas as pl
from jax.experimental.pallas import tpu as pltpu
from jax.sharding import PartitionSpec as P

MESH = pl.DeviceIdType.MESH
F32 = jnp.float32
BF16 = jnp.bfloat16
I32 = jnp.int32

D = 6400
HID = 640
SLOTS = 256
TOK = 128
BLK = 400
HALF_A = 208
NZ = 8


def al(value, multiple):
    return pl.multiple_of(value, multiple)


def kernel(
    tokens,
    ids,
    gate_w,
    gu_codes,
    gu_scales,
    dn_codes,
    dn_scales,
    sgu_codes,
    sgu_scales,
    sdn_codes,
    sdn_scales,
    out,
    rgu,
    rdn,
    gu_all,
    dn_all,
    weights,
    wdown,
    xs_t,
    xs,
    tk_t,
    tk,
    acc_g,
    acc_u,
    hidden,
    hidden_sh,
    part_r,
    part_s,
    sib_r,
    sib_s,
    psend_r,
    precv_r,
    msend_r,
    mrecv_r,
    psend_s,
    precv_s,
    msend_s,
    mrecv_s,
    select,
    disp,
    disp_in,
    back,
    back_in,
    own_r,
    own_s,
    wsend,
    wrecv,
    zsend,
    zrecv,
    asend,
    arecv,
    rsend,
    rrecv,
    lsem,
):
    core = lax.axis_index("seq")
    exp = lax.axis_index("expert")
    z = lax.axis_index("tensor")
    ex = exp // 4
    ey = lax.rem(exp, 4)
    other = 1 - core
    zplus = lax.rem(z + 1, NZ)
    zminus = lax.rem(z + NZ - 1, NZ)

    local_gu = []
    for b in range(10):
        rows = pl.ds(128 * b, 128)
        cp = pltpu.make_async_copy(gu_codes.at[:, rows, :], rgu.at[:, rows, :], lsem.at[b])
        cp.start()
        local_gu.append(cp)
    local_dn = pltpu.make_async_copy(dn_codes, rdn, lsem.at[10])
    local_own = pltpu.make_async_copy(
        sgu_codes, gu_all.at[:, pl.ds(al(80 * exp, 80), 80), :], lsem.at[11]
    )
    local_own.start()
    local_dn.start()

    barrier = pltpu.get_barrier_semaphore()

    def greet(k, _):
        pl.semaphore_signal(
            barrier, inc=1, device_id={"expert": lax.rem(exp + k, 16)}, device_id_type=MESH
        )
        return 0

    lax.fori_loop(1, 16, greet, 0)
    pl.semaphore_signal(barrier, inc=1, device_id={"seq": other}, device_id_type=MESH)
    pl.semaphore_signal(barrier, inc=1, device_id={"tensor": zplus}, device_id_type=MESH)
    pl.semaphore_signal(barrier, inc=1, device_id={"tensor": zminus}, device_id_type=MESH)
    pl.semaphore_wait(barrier, 18)

    sent = []

    def copy(src, dst, ssem, rsem, device):
        return pltpu.make_async_remote_copy(
            src_ref=src,
            dst_ref=dst,
            send_sem=ssem,
            recv_sem=rsem,
            device_id=device,
            device_id_type=MESH,
        )

    def push(src, dst, ssem, rsem, device):
        cp = copy(src, dst, ssem, rsem, device)
        cp.start()
        sent.append(cp)

    def region(piece, ee, half):
        if piece < 2:
            off, size = ((0, 80), (0, 40), (40, 40))[half]
            return gu_all.at[piece, pl.ds(al(80 * ee + off, 8), size), :]
        base = 200 * (piece - 2)
        off, size = ((0, 200), (0, 104), (104, 96))[half]
        return dn_all.at[pl.ds(al(400 * ee + (base + off), 8), size), :]

    class Piece:
        def __init__(self, piece):
            self.piece = piece
            self.by_x = piece % 2 == 0
            self.a = ex if self.by_x else ey
            self.b = ey if self.by_x else ex

        def block(self, da, db):
            a = lax.rem(self.a + da + 4, 4)
            b = lax.rem(self.b + db + 4, 4)
            return a * 4 + b if self.by_x else b * 4 + a

        def send(self, sem, da, db, half, step_a, step_b):
            ref = region(self.piece, self.block(da, db), half)
            s = 20 * self.piece + sem
            push(ref, ref, wsend.at[s], wrecv.at[s], {"expert": self.block(step_a, step_b)})

        def wait(self, sem, da, db, half):
            ref = region(self.piece, self.block(da, db), half)
            s = 20 * self.piece + sem
            copy(ref, ref, wsend.at[s], wrecv.at[s], {"expert": self.block(1, 0)}).wait_recv()

        def stage2(self, q, da):
            self.send(4 + 4 * q, da, 0, 0, 0, 1)
            self.send(5 + 4 * q, da, 0, 0, 0, -1)

        def stage2_forward(self, q, da):
            self.wait(4 + 4 * q, da, -1, 0)
            self.send(6 + 4 * q, da, -1, 1, 0, 1)
            self.wait(5 + 4 * q, da, 1, 0)
            self.send(7 + 4 * q, da, 1, 2, 0, -1)

        def stage2_end(self, q, da):
            self.wait(6 + 4 * q, da, 2, 1)
            self.wait(7 + 4 * q, da, 2, 2)

        def r0(self):
            self.send(0, 0, 0, 0, 1, 0)
            self.send(1, 0, 0, 0, -1, 0)
            self.stage2(0, 0)

        def r1(self):
            self.wait(0, -1, 0, 0)
            self.send(2, -1, 0, 1, 1, 0)
            self.stage2(1, -1)
            self.wait(1, 1, 0, 0)
            self.send(3, 1, 0, 2, -1, 0)
            self.stage2(2, 1)
            self.stage2_forward(0, 0)

        def r2(self):
            self.wait(2, 2, 0, 1)
            self.wait(3, 2, 0, 2)
            self.stage2(3, 2)
            self.stage2_forward(1, -1)
            self.stage2_forward(2, 1)
            self.stage2_end(0, 0)

        def r3(self):
            self.stage2_forward(3, 2)
            self.stage2_end(1, -1)
            self.stage2_end(2, 1)

        def r4(self):
            self.stage2_end(3, 2)

        def arrived(self, r):
            return (
                ((0, 0),),
                ((-1, 0), (1, 0), (0, -1), (0, 1)),
                ((2, 0), (-1, -1), (-1, 1), (1, -1), (1, 1), (0, 2)),
                ((2, -1), (2, 1), (-1, 2), (1, 2)),
                ((2, 2),),
            )[r]

    gate, up, down_a, down_b = (Piece(i) for i in range(4))

    class Gather:
        def __init__(self, ref, which):
            self.ref = ref
            self.base = 17 * which

        def rows(self, c, dz, part):
            off, size = ((0, BLK), (0, HALF_A), (HALF_A, BLK - HALF_A))[part]
            start = 3200 * c + BLK * lax.rem(z + dz + NZ, NZ) + off
            return self.ref.at[pl.ds(al(start, 16), size), :]

        def to_plus(self, s, dz, part):
            ref = self.rows(core, dz, part)
            push(ref, ref, zsend.at[self.base + s], zrecv.at[self.base + s], {"tensor": zplus})

        def to_minus(self, s, dz, part):
            ref = self.rows(core, dz, part)
            k = self.base + 4 + s
            push(ref, ref, zsend.at[k], zrecv.at[k], {"tensor": zminus})

        def to_sibling(self, s, dz, part):
            ref = self.rows(core, dz, part)
            k = self.base + 8 + s
            push(ref, ref, zsend.at[k], zrecv.at[k], {"seq": other})

        def wait(self, s, c, dz, part):
            ref = self.rows(c, dz, part)
            k = self.base + s
            copy(ref, ref, zsend.at[k], zrecv.at[k], {"seq": other}).wait_recv()

        def r0(self):
            self.to_plus(0, 0, 0)
            self.to_minus(0, 0, 0)
            self.to_sibling(0, 0, 0)

        def step(self, r):
            part = 0 if r < 3 else 1
            self.wait(r - 1, core, -r, 0)
            self.to_plus(r, -r, part)
            self.wait(4 + r - 1, core, r, 0)
            self.to_minus(r, r, 0 if r < 3 else 2)
            self.to_sibling(2 * r - 1, -r, 0)
            self.to_sibling(2 * r, r, 0)

        def last(self):
            self.wait(3, core, 4, 1)
            self.to_sibling(7, 4, 1)
            self.wait(7, core, 4, 2)
            self.to_sibling(8, 4, 2)
            self.wait(8, other, 0, 0)
            for r in (1, 2, 3):
                self.wait(8 + 2 * r - 1, other, -r, 0)
                self.wait(8 + 2 * r, other, r, 0)
            self.wait(15, other, 4, 1)
            self.wait(16, other, 4, 2)

    slots = Gather(xs_t, 0)
    toks = Gather(tk_t, 1)

    class Scatter:
        def __init__(self, which, part, sib, psend, precv, msend, mrecv):
            self.base = 9 * which
            self.part, self.sib = part, sib
            self.psend, self.precv, self.msend, self.mrecv = psend, precv, msend, mrecv

        def begin(self):
            src = self.part.at[pl.ds(al(3200 * other, 16), 3200), :]
            k = self.base
            push(src, self.sib, rsend.at[k], rrecv.at[k], {"seq": other})

        def begin_wait(self):
            k = self.base
            copy(self.sib, self.sib, rsend.at[k], rrecv.at[k], {"seq": other}).wait_recv()

        def pair(self, dz, lo, size):
            d = lax.rem(z + dz + NZ, NZ)
            mine = self.part[pl.ds(al(3200 * core + BLK * d + lo, 16), size), :]
            theirs = self.sib[pl.ds(al(BLK * d + lo, 16), size), :]
            return mine.astype(F32) + theirs.astype(F32)

        def go(self, s, lo, size):
            rows = pl.ds(lo, size)
            k = self.base + 1 + s
            push(self.psend.at[s, rows, :], self.precv.at[s, rows, :], rsend.at[k], rrecv.at[k],
                 {"tensor": zplus})

        def go_minus(self, s, lo, size):
            rows = pl.ds(lo, size)
            k = self.base + 5 + s
            push(self.msend.at[s, rows, :], self.mrecv.at[s, rows, :], rsend.at[k], rrecv.at[k],
                 {"tensor": zminus})

        def wait_plus(self, s, lo, size):
            ref = self.precv.at[s, pl.ds(lo, size), :]
            k = self.base + 1 + s
            copy(ref, ref, rsend.at[k], rrecv.at[k], {"tensor": zplus}).wait_recv()

        def wait_minus(self, s, lo, size):
            ref = self.mrecv.at[s, pl.ds(lo, size), :]
            k = self.base + 5 + s
            copy(ref, ref, rsend.at[k], rrecv.at[k], {"tensor": zminus}).wait_recv()

        def s0(self):
            rest = BLK - HALF_A
            self.psend[0, 0:HALF_A, :] = self.pair(4, 0, HALF_A).astype(BF16)
            self.go(0, 0, HALF_A)
            self.msend[0, HALF_A:BLK, :] = self.pair(4, HALF_A, rest).astype(BF16)
            self.go_minus(0, HALF_A, rest)

        def s1(self):
            rest = BLK - HALF_A
            self.psend[1, HALF_A:BLK, :] = self.pair(3, HALF_A, rest).astype(BF16)
            self.msend[1, 0:HALF_A, :] = self.pair(-3, 0, HALF_A).astype(BF16)
            self.wait_plus(0, 0, HALF_A)
            got = self.precv[0, 0:HALF_A, :].astype(F32)
            self.psend[1, 0:HALF_A, :] = (self.pair(3, 0, HALF_A) + got).astype(BF16)
            self.go(1, 0, BLK)
            self.wait_minus(0, HALF_A, rest)
            got = self.mrecv[0, HALF_A:BLK, :].astype(F32)
            self.msend[1, HALF_A:BLK, :] = (self.pair(-3, HALF_A, rest) + got).astype(BF16)
            self.go_minus(1, 0, BLK)

        def step(self, s):
            self.wait_plus(s - 1, 0, BLK)
            got = self.precv[s - 1].astype(F32)
            self.psend[s] = (self.pair(4 - s, 0, BLK) + got).astype(BF16)
            self.go(s, 0, BLK)
            self.wait_minus(s - 1, 0, BLK)
            got = self.mrecv[s - 1].astype(F32)
            self.msend[s] = (self.pair(s - 4, 0, BLK) + got).astype(BF16)
            self.go_minus(s, 0, BLK)

        def end(self):
            self.wait_plus(3, 0, BLK)
            self.wait_minus(3, 0, BLK)
            return (
                self.pair(0, 0, BLK)
                + self.precv[3].astype(F32)
                + self.mrecv[3].astype(F32)
            )

    sum_r = Scatter(0, part_r, sib_r, psend_r, precv_r, msend_r, mrecv_r)
    sum_s = Scatter(1, part_s, sib_s, psend_s, precv_s, msend_s, mrecv_s)

    def unpack_strip(words, scale_rows, store):
        w = words.astype(I32) ^ 0x88888
        for k in range(5):
            shift = 28 - 4 * k
            code = lax.shift_right_arithmetic(lax.shift_left(w, I32(shift)), I32(28))
            store(k, (code.astype(F32) * scale_rows[k]).astype(BF16))

    def unpack_gu(codes, scales, m, strip):
        b = strip // 8
        inner = lax.rem(strip, 8) * 16
        rows = [scales[m, pl.ds(5 * b + k, 1), :] for k in range(5)]

        def store(k, value):
            weights[m, pl.ds(al((5 * b + k) * 128 + inner, 16), 16), :] = value

        unpack_strip(codes[m, pl.ds(al(strip * 16, 16), 16), :], rows, store)

    def unpack_routed(b):
        local_gu[b].wait()

        def one(i, _):
            unpack_gu(rgu, gu_scales, i // 8, 8 * b + lax.rem(i, 8))
            return 0

        lax.fori_loop(0, 16, one, 0)

    def unpack_shared(piece, r):
        for da, db in piece.arrived(r):
            ee = piece.block(da, db)

            def one(i, _):
                unpack_gu(gu_all, sgu_scales, piece.piece, 5 * ee + i)
                return 0

            lax.fori_loop(0, 5, one, 0)

    def transpose_in(src, dst):
        def one(i, _):
            at = al(i * 256, 256)
            dst[:, pl.ds(at, 256)] = src[pl.ds(at, 256), :].T
            return 0

        lax.fori_loop(0, 25, one, 0)

    def hidden_units(rows, x, target):
        zero = jnp.zeros((rows, HID), F32)
        acc_g[0:rows, :] = zero
        acc_u[0:rows, :] = zero

        def one(i, _):
            at = pl.ds(al(i * 640, 640), 640)
            xk = x[:, at]
            acc_g[0:rows, :] += jnp.dot(xk, weights[0, at, :], preferred_element_type=F32)
            acc_u[0:rows, :] += jnp.dot(xk, weights[1, at, :], preferred_element_type=F32)
            return 0

        lax.fori_loop(0, 10, one, 0)
        g = acc_g[0:rows, :]
        target[...] = (g / (1.0 + jnp.exp(-g)) * acc_u[0:rows, :]).astype(BF16)

    def down(words_of, scales, h, target, lo, hi):
        def one(j, _):
            cols = pl.ds(al(j * 640, 640), 640)

            def strip(i, _):
                rows = [scales[pl.ds(k, 1), cols] for k in range(5)]

                def store(k, value):
                    wdown[pl.ds(al(k * 128 + i * 16, 16), 16), :] = value

                unpack_strip(words_of(i, j), rows, store)
                return 0

            lax.fori_loop(0, 8, strip, 0)
            y = jnp.dot(h[...], wdown[...], preferred_element_type=F32).astype(BF16)
            target[cols, :] = y.T
            return 0

        lax.fori_loop(lo, hi, one, 0)

    local_own.wait()
    gate.r0()
    up.r0()

    expert_row = ids[...]
    onehot = (lax.broadcasted_iota(I32, (16, TOK), 0) == expert_row).astype(F32)
    upto = (
        lax.broadcasted_iota(I32, (TOK, TOK), 0) <= lax.broadcasted_iota(I32, (TOK, TOK), 1)
    ).astype(BF16)
    counted = jnp.dot(onehot.astype(BF16), upto, preferred_element_type=F32)
    rank = jnp.sum(counted * onehot, axis=0, keepdims=True) - 1.0
    slot = expert_row.astype(F32) * 16.0 + rank
    chosen = lax.broadcasted_iota(I32, (SLOTS, TOK), 0).astype(F32) == slot
    select[...] = chosen.astype(F32).astype(BF16)
    tok = tokens[...]
    disp[...] = jnp.dot(select[...], tok, preferred_element_type=F32).astype(BF16)

    def a2a(src, dst, k):
        def one(i, _):
            to = lax.rem(exp + i, 16)
            copy(
                src.at[pl.ds(al(16 * to, 16), 16), :],
                dst.at[pl.ds(al(16 * exp, 16), 16), :],
                asend.at[k],
                arecv.at[k],
                {"expert": to},
            ).start()
            return 0

        lax.fori_loop(1, 16, one, 0)
        mine = pl.ds(al(16 * exp, 16), 16)
        dst[mine, :] = src[mine, :]

    def a2a_wait(dst, k):
        ref = dst.at[pl.ds(0, 240), :]
        copy(ref, ref, asend.at[k], arecv.at[k], {"seq": other}).wait_recv()

    def a2a_end(src, k):
        ref = src.at[pl.ds(0, 240), :]
        copy(ref, ref, asend.at[k], arecv.at[k], {"seq": other}).wait_send()

    own_rows = pl.ds(al(3200 * core + BLK * z, 16), BLK)
    a2a(disp, disp_in, 0)
    tk_t[own_rows, :] = tok.T
    toks.r0()
    dn_all[pl.ds(al(400 * exp, 8), 400), :] = sdn_codes[...].T

    unpack_routed(0)
    unpack_routed(1)
    a2a_wait(disp_in, 0)
    xs_t[own_rows, :] = disp_in[...].T
    slots.r0()

    unpack_routed(2)
    toks.step(1)
    unpack_routed(3)
    gate.r1()
    up.r1()
    unpack_routed(4)
    slots.step(1)
    unpack_routed(5)
    unpack_routed(6)
    toks.step(2)
    unpack_routed(7)
    slots.step(2)
    unpack_routed(8)
    unpack_routed(9)
    slots.step(3)
    toks.step(3)
    gate.r2()
    up.r2()
    down_a.r0()
    down_b.r0()
    slots.last()
    transpose_in(xs_t, xs)
    hidden_units(SLOTS, xs, hidden)
    toks.last()

    local_dn.wait()

    def routed_words(i, j):
        return rdn[pl.ds(al(i * 16, 16), 16), pl.ds(al(j * 640, 640), 640)]

    down(routed_words, dn_scales, hidden, part_r, 0, 10)
    sum_r.begin()
    for r in (0, 1):
        unpack_shared(gate, r)
        unpack_shared(up, r)
    sum_r.begin_wait()
    sum_r.s0()
    unpack_shared(gate, 2)
    unpack_shared(up, 2)
    gate.r3()
    up.r3()
    down_a.r1()
    down_b.r1()
    sum_r.s1()
    unpack_shared(gate, 3)
    unpack_shared(up, 3)
    sum_r.step(2)
    gate.r4()
    up.r4()
    down_a.r2()
    down_b.r2()
    unpack_shared(gate, 4)
    unpack_shared(up, 4)
    transpose_in(tk_t, tk)
    hidden_units(TOK, tk, hidden_sh)
    sum_r.step(3)
    down_a.r3()
    down_b.r3()
    down_a.r4()
    down_b.r4()
    back[...] = sum_r.end().astype(BF16).T
    a2a(back, back_in, 1)

    def shared_words_at(j):
        rows = pl.ds(al(j * 640, 640), 640)
        rdn[:, rows] = dn_all[rows, :].T

    def turn(j, _):
        shared_words_at(j)
        return 0

    lax.fori_loop(0, 10, turn, 0)
    down(routed_words, sdn_scales, hidden_sh, part_s, 0, 10)
    sum_s.begin()
    sum_s.begin_wait()
    sum_s.s0()
    sum_s.s1()
    sum_s.step(2)
    sum_s.step(3)
    a2a_wait(back_in, 1)
    routed = lax.dot_general(
        select[...], back_in[...], (((0,), (0,)), ((), ())), preferred_element_type=F32
    )
    diag = lax.broadcasted_iota(I32, (TOK, TOK), 0) == lax.broadcasted_iota(I32, (TOK, TOK), 1)
    factor = jnp.sum(jnp.where(diag, gate_w[...], 0.0), axis=1, keepdims=True)
    shared = sum_s.end().T
    out[...] = (shared + factor * routed).astype(BF16)

    a2a_end(disp, 0)
    a2a_end(back, 1)
    for cp in sent:
        cp.wait_send()


def shards(
    tokens,
    expert_ids,
    gate_weights,
    gate_up_codes,
    gate_up_scales,
    down_codes,
    down_scales,
    shared_gate_up_codes,
    shared_gate_up_scales,
    shared_down_codes,
    shared_down_scales,
):
    vmem = pl.BlockSpec(memory_space=pltpu.VMEM)
    hbm = pl.BlockSpec(memory_space=pl.ANY)
    V = pltpu.VMEM
    S = pltpu.SemaphoreType.DMA
    return pl.pallas_call(
        kernel,
        out_shape=jax.ShapeDtypeStruct((TOK, BLK), BF16),
        in_specs=[vmem, vmem, vmem, hbm, vmem, hbm, vmem, hbm, vmem, vmem, vmem],
        out_specs=vmem,
        scratch_shapes=[
            V((2, 1280, HID), F32),
            V((128, D), F32),
            V((2, 1280, HID), F32),
            V((D, 128), F32),
            V((2, D, HID), BF16),
            V((HID, HID), BF16),
            V((D, SLOTS), BF16),
            V((SLOTS, D), BF16),
            V((D, TOK), BF16),
            V((TOK, D), BF16),
            V((SLOTS, HID), F32),
            V((SLOTS, HID), F32),
            V((SLOTS, HID), BF16),
            V((TOK, HID), BF16),
            V((D, SLOTS), BF16),
            V((D, TOK), BF16),
            V((3200, SLOTS), BF16),
            V((3200, TOK), BF16),
            V((4, BLK, SLOTS), BF16),
            V((4, BLK, SLOTS), BF16),
            V((4, BLK, SLOTS), BF16),
            V((4, BLK, SLOTS), BF16),
            V((4, BLK, TOK), BF16),
            V((4, BLK, TOK), BF16),
            V((4, BLK, TOK), BF16),
            V((4, BLK, TOK), BF16),
            V((SLOTS, TOK), BF16),
            V((SLOTS, BLK), BF16),
            V((SLOTS, BLK), BF16),
            V((SLOTS, BLK), BF16),
            V((SLOTS, BLK), BF16),
            V((8, 128), F32),
            V((8, 128), F32),
            S((80,)),
            S((80,)),
            S((34,)),
            S((34,)),
            S((2,)),
            S((2,)),
            S((18,)),
            S((18,)),
            S((12,)),
        ],
        compiler_params=pltpu.CompilerParams(
            collective_id=0, has_side_effects=True, vmem_limit_bytes=64 * 1024 * 1024 - 65536
        ),
    )(
        tokens,
        expert_ids.reshape(1, TOK),
        gate_weights.reshape(1, TOK),
        gate_up_codes[0],
        gate_up_scales[0],
        down_codes[0],
        down_scales[0],
        shared_gate_up_codes,
        shared_gate_up_scales,
        shared_down_codes,
        shared_down_scales,
    )


def solution(mesh):
    placed = (
        P("expert", ("seq", "tensor")),
        P("expert"),
        P("expert"),
        P("expert", None, None, ("seq", "tensor")),
        P("expert", None, None, ("seq", "tensor")),
        P("expert", ("seq", "tensor"), None),
        P("expert", ("seq", "tensor"), None),
        P(None, "expert", ("seq", "tensor")),
        P(None, None, ("seq", "tensor")),
        P(("seq", "tensor"), "expert"),
        P(("seq", "tensor"), None),
    )
    return jax.shard_map(
        shards,
        mesh=mesh,
        in_specs=placed,
        out_specs=P("expert", ("seq", "tensor")),
        check_vma=False,
    )
```

profile of v0, /device:TPU:1, one launch (start us, length us, event | category | flops | bytes accessed | tf_op | source)
XLA Modules:
  0.0 143.1 jit_solution(880932415227234879)
XLA Ops:
  0.0 1.6 %copy.13.tokens = bf16[128,400]{1,0:T(8,128)(2,1)} copy(bf16[128,400]{0,1:T(8,128)(2,1)} %param.11) | data formatting | bytes 204800 | tf_op args[0]
  1.7 1.6 %copy.21 = f32[1,5,6400]{2,1,0:T(8,128)} copy(f32[1,5,6400]{2,0,1:T(1,128)} %param.17) | data formatting | bytes 256000
  3.3 1.8 %copy.15.sdn_codes = f32[128,400]{1,0:T(8,128)} copy(f32[128,400]{0,1:T(8,128)} %param.20) | data formatting | bytes 409600 | tf_op args[9]
  5.0 1.7 %copy.20 = f32[1,2,50,640]{3,2,1,0:T(8,128)} copy(f32[1,2,50,640]{3,1,2,0:T(2,128)} %param.15) | data formatting | bytes 512000 | tf_op args[4]
  6.7 1.7 %copy.14.sgu_scales = f32[2,50,640]{2,1,0:T(8,128)} copy(f32[2,50,640]{2,0,1:T(2,128)} %param.19) | data formatting | bytes 512000 | tf_op args[8]
  8.4 133.1 %shard_map.109 = bf16[128,400]{1,0:T(8,128)(2,1)} custom-call(bf16[128,400]{1,0:T(8,128)(2,1)} %copy.13.tokens, s32[1,128]{1,0:T(1,128)} %bitcast.14, f32[1,128]{1,0:T(1,128)} %bitcast.15, f32[2,1280,640]{2,1,0:T(8,128)} %bitcast.10, f32[2,50,640]{2,1,0:T(8,128)} %bitcast.12, f32[128,6400]{1,0:T(8,128)} %bitcast.11, f32[5,6400]{1,0:T(8,128)} %bitcast.13, ...), custom_call_target="tpu_custom_call" | custom-call | tf_op jit(solution)/shard_map/pallas_call | solution.py:609
  141.4 1.7 %copy.16 = bf16[128,400]{0,1:T(8,128)(2,1)} copy(bf16[128,400]{1,0:T(8,128)(2,1)} %shard_map.109) | data formatting | bytes 204800 | tf_op jit(solution)/shard_map/pallas_call | solution.py:609
where the time goes:
time: 144 us; the launch traced here: 143 us
  Pallas kernels  133 us (92%)
  local copies, waits for them, and re-layouts  10 us (7%)
    pallas_call x1, Pallas kernels, shards(): pl.pallas_call(kernel, out_shape=jax.ShapeDtypeStruct((TOK, BLK), BF16),...  133 us
    unnamed x5, local copies, waits for them, and re-layouts  8.36 us

commit v1 on v0

v1 whole, which is shorter than its diff:
```python
import jax
import jax.numpy as jnp
from jax import lax
from jax.experimental import pallas as pl
from jax.experimental.pallas import tpu as pltpu
from jax.sharding import PartitionSpec as P

MESH = pl.DeviceIdType.MESH
F32 = jnp.float32
BF16 = jnp.bfloat16
I32 = jnp.int32

D = 6400
HID = 640
SLOTS = 256
TOK = 128
BLK = 400
PARTS = ((0, 208), (208, 192), (0, 400))
NZ = 8


def al(value, multiple):
    return pl.multiple_of(value, multiple)


def pick(j, values):
    chosen = values[0]
    for k in range(1, len(values)):
        chosen = lax.select(j == k, values[k], chosen)
    return chosen


def kernel(
    tokens,
    ids_in,
    gate_in,
    gu_codes,
    gu_scales_in,
    dn_codes,
    dn_scales_in,
    sgu_codes,
    sgu_scales_in,
    sdn_codes,
    sdn_scales_in,
    out,
    ids,
    gate_w,
    gu_scales,
    dn_scales,
    sgu_scales,
    sdn_scales,
    scale_rows,
    scale_cols,
    rgu,
    rdn,
    rdn_t,
    gu_all,
    dn_all,
    weights,
    wshard,
    wdown,
    xs_t,
    tk_t,
    xperm,
    acc_r,
    acc_s,
    hid_r,
    hid_s,
    part_r,
    part_s,
    sib_r,
    sib_s,
    precv_r,
    mrecv_r,
    precv_s,
    mrecv_s,
    select,
    disp,
    disp_in,
    back,
    back_in,
    wsend,
    wrecv,
    zsend,
    zrecv,
    asend,
    arecv,
    rsend,
    rrecv,
    lsem,
):
    core = lax.axis_index("seq")
    exp = lax.axis_index("expert")
    z = lax.axis_index("tensor")
    ex = exp // 4
    ey = lax.rem(exp, 4)
    other = 1 - core
    zplus = lax.rem(z + 1, NZ)
    zminus = lax.rem(z + NZ - 1, NZ)

    barrier = pltpu.get_barrier_semaphore()

    def greet(k, _):
        pl.semaphore_signal(
            barrier, inc=1, device_id={"expert": lax.rem(exp + k, 16)}, device_id_type=MESH
        )
        return 0

    pl.semaphore_signal(barrier, inc=1, device_id={"seq": other}, device_id_type=MESH)
    pl.semaphore_signal(barrier, inc=1, device_id={"tensor": zplus}, device_id_type=MESH)
    pl.semaphore_signal(barrier, inc=1, device_id={"tensor": zminus}, device_id_type=MESH)
    lax.fori_loop(1, 16, greet, 0)

    def load(src, dst, k):
        cp = pltpu.make_async_copy(src, dst, lsem.at[k])
        cp.start()
        return cp

    own_rows = pl.ds(al(3200 * core + BLK * z, 16), BLK)
    dn_rows = pl.ds(al(BLK * exp, 16), BLK)
    local_tok = load(tokens, tk_t.at[own_rows, :], 0)
    local_ids = load(ids_in, ids, 1)
    local_gate = load(gate_in, gate_w, 2)
    local_sgu = load(sgu_codes, gu_all.at[:, pl.ds(al(80 * exp, 8), 80), :], 3)
    local_sdn = load(sdn_codes, dn_all.at[dn_rows, :], 4)
    local_gs = load(gu_scales_in, gu_scales, 5)
    local_gu = []
    for b in range(10):
        rows = pl.ds(128 * b, 128)
        local_gu.append(load(gu_codes.at[:, rows, :], rgu.at[:, rows, :], 10 + b))
    local_dn = load(dn_codes, rdn, 6)
    local_ds = load(dn_scales_in, dn_scales, 7)
    local_ss = load(sgu_scales_in, sgu_scales, 8)
    local_sds = load(sdn_scales_in, sdn_scales, 9)

    sent = []

    def copy(src, dst, ssem, rsem, device):
        return pltpu.make_async_remote_copy(
            src_ref=src,
            dst_ref=dst,
            send_sem=ssem,
            recv_sem=rsem,
            device_id=device,
            device_id_type=MESH,
        )

    def push(src, dst, ssem, rsem, device):
        cp = copy(src, dst, ssem, rsem, device)
        cp.start()
        sent.append(cp)

    def region(piece, ee, half):
        if piece < 2:
            off, size = ((0, 80), (0, 40), (40, 40))[half]
            return gu_all.at[piece, pl.ds(al(80 * ee + off, 8), size), :]
        base = 200 * (piece - 2)
        off, size = ((0, 200), (0, 104), (104, 96))[half]
        return dn_all.at[pl.ds(al(400 * ee + (base + off), 8), size), :]

    class Piece:
        def __init__(self, piece):
            self.piece = piece
            self.by_x = piece % 2 == 0
            self.a = ex if self.by_x else ey
            self.b = ey if self.by_x else ex

        def block(self, da, db):
            a = lax.rem(self.a + da + 4, 4)
            b = lax.rem(self.b + db + 4, 4)
            return a * 4 + b if self.by_x else b * 4 + a

        def send(self, sem, da, db, half, step_a, step_b):
            ref = region(self.piece, self.block(da, db), half)
            s = 20 * self.piece + sem
            push(ref, ref, wsend.at[s], wrecv.at[s], {"expert": self.block(step_a, step_b)})

        def wait(self, sem, da, db, half):
            ref = region(self.piece, self.block(da, db), half)
            s = 20 * self.piece + sem
            copy(ref, ref, wsend.at[s], wrecv.at[s], {"expert": self.block(1, 0)}).wait_recv()

        def stage2(self, q, da):
            self.send(4 + 4 * q, da, 0, 0, 0, 1)
            self.send(5 + 4 * q, da, 0, 0, 0, -1)

        def stage2_forward(self, q, da):
            self.wait(4 + 4 * q, da, -1, 0)
            self.send(6 + 4 * q, da, -1, 1, 0, 1)
            self.wait(5 + 4 * q, da, 1, 0)
            self.send(7 + 4 * q, da, 1, 2, 0, -1)

        def stage2_end(self, q, da):
            self.wait(6 + 4 * q, da, 2, 1)
            self.wait(7 + 4 * q, da, 2, 2)

        def r0(self):
            self.send(0, 0, 0, 0, 1, 0)
            self.send(1, 0, 0, 0, -1, 0)
            self.stage2(0, 0)

        def r1(self):
            self.wait(0, -1, 0, 0)
            self.send(2, -1, 0, 1, 1, 0)
            self.stage2(1, -1)
            self.wait(1, 1, 0, 0)
            self.send(3, 1, 0, 2, -1, 0)
            self.stage2(2, 1)
            self.stage2_forward(0, 0)

        def r2(self):
            self.wait(2, 2, 0, 1)
            self.wait(3, 2, 0, 2)
            self.stage2(3, 2)
            self.stage2_forward(1, -1)
            self.stage2_forward(2, 1)
            self.stage2_end(0, 0)

        def r3(self):
            self.stage2_forward(3, 2)
            self.stage2_end(1, -1)
            self.stage2_end(2, 1)

        def r4(self):
            self.stage2_end(3, 2)

        def arrived(self, r):
            places = (
                ((0, 0),),
                ((-1, 0), (1, 0), (0, -1), (0, 1)),
                ((2, 0), (0, 2), (-1, -1), (-1, 1), (1, -1), (1, 1)),
                ((2, -1), (2, 1), (-1, 2), (1, 2)),
                ((2, 2),),
            )[r]
            return [self.block(da, db) for da, db in places]

    gate, up, down_a, down_b = (Piece(i) for i in range(4))

    def block_of(c, dz):
        return NZ * c + lax.rem(z + dz + NZ, NZ)

    class Gather:
        def __init__(self, ref, which):
            self.ref = ref
            self.base = 32 * which

        def rows(self, c, dz, part):
            off, size = PARTS[part]
            return self.ref.at[pl.ds(al(BLK * block_of(c, dz) + off, 16), size), :]

        def ring(self, up_way, r, part):
            ref = self.rows(core, -r if up_way else r, part)
            k = self.base + (0 if up_way else 8) + 2 * r + part
            to = zplus if up_way else zminus
            push(ref, ref, zsend.at[k], zrecv.at[k], {"tensor": to})

        def sibling(self, dz, part):
            ref = self.rows(core, dz, part)
            k = self.base + 16 + 2 * (dz % NZ) + part
            push(ref, ref, zsend.at[k], zrecv.at[k], {"seq": other})

        def ring_wait(self, up_way, r, part):
            ref = self.rows(core, -r if up_way else r, part)
            k = self.base + (0 if up_way else 8) + 2 * (r - 1) + part
            copy(ref, ref, zsend.at[k], zrecv.at[k], {"tensor": zplus}).wait_recv()

        def sibling_wait(self, dz):
            for part in (0, 1):
                ref = self.rows(other, dz, part)
                k = self.base + 16 + 2 * (dz % NZ) + part
                copy(ref, ref, zsend.at[k], zrecv.at[k], {"seq": other}).wait_recv()

        def r0(self):
            for part in (0, 1):
                self.ring(True, 0, part)
                self.ring(False, 0, part)
            for part in (0, 1):
                self.sibling(0, part)

        def step(self, r):
            for part in (0, 1):
                for up_way in (True, False):
                    long_way = (part == 0) == up_way
                    if r == 4 and not long_way:
                        continue
                    self.ring_wait(up_way, r, part)
                    if r <= (3 if long_way else 2):
                        self.ring(up_way, r, part)
                    self.sibling(-r if up_way else r, part)

    slots = Gather(xs_t, 0)
    toks = Gather(tk_t, 1)

    class Scatter:
        def __init__(self, which, part, sib, precv, mrecv):
            self.base = 24 * which
            self.part, self.sib = part, sib
            self.recv = (precv, mrecv)

        def to_sibling(self, d):
            rows = pl.ds(al(BLK * (NZ * other + d), 16), BLK)
            k = self.base + d
            push(
                self.part.at[rows, :],
                self.sib.at[pl.ds(al(BLK * d, 16), BLK), :],
                rsend.at[k],
                rrecv.at[k],
                {"seq": other},
            )

        def sibling_wait(self, d):
            ref = self.sib.at[pl.ds(al(BLK * d, 16), BLK), :]
            k = self.base + d
            copy(ref, ref, rsend.at[k], rrecv.at[k], {"seq": other}).wait_recv()

        def pair(self, d, part):
            lo, size = PARTS[part]
            mine = self.part[pl.ds(al(BLK * (NZ * core + d) + lo, 16), size), :]
            theirs = self.sib[pl.ds(al(BLK * d + lo, 16), size), :]
            return mine.astype(F32) + theirs.astype(F32)

        def slot(self, way, s, part):
            lo, size = PARTS[part]
            return self.recv[way].at[s, pl.ds(lo, size), :]

        def wait(self, way, s, part):
            ref = self.slot(way, s, part)
            k = self.base + 8 + 8 * way + 2 * s + part
            copy(ref, ref, rsend.at[k], rrecv.at[k], {"tensor": zplus}).wait_recv()

        def message(self, way, s, part):
            lo, size = PARTS[part]
            d = lax.rem(z + (4 - s if way == 0 else s - 4) + NZ, NZ)
            value = self.pair(d, part)
            if s > (0 if way == part else 1):
                self.wait(way, s - 1, part)
                value = value + self.recv[way][s - 1, pl.ds(lo, size), :].astype(F32)
            rows = pl.ds(al(BLK * (NZ * core + d) + lo, 16), size)
            self.part[rows, :] = value.astype(BF16)
            k = self.base + 8 + 8 * way + 2 * s + part
            push(
                self.part.at[rows, :],
                self.slot(way, s, part),
                rsend.at[k],
                rrecv.at[k],
                {"tensor": zplus if way == 0 else zminus},
            )

        def step(self, s):
            if s == 0:
                self.message(0, 0, 0)
                self.message(1, 0, 1)
                return
            if s == 1:
                self.message(0, 1, 1)
                self.message(1, 1, 0)
                self.message(0, 1, 0)
                self.message(1, 1, 1)
                return
            for part in (0, 1):
                self.message(part, s, 1 - part)
            for part in (0, 1):
                self.message(part, s, part)

        def end(self):
            for way in (0, 1):
                for part in (0, 1):
                    self.wait(way, 3, part)
            return (
                self.pair(z, 2)
                + self.recv[0][3].astype(F32)
                + self.recv[1][3].astype(F32)
            )

    sum_r = Scatter(0, part_r, sib_r, precv_r, mrecv_r)
    sum_s = Scatter(1, part_s, sib_s, precv_s, mrecv_s)

    def digits(words, scale_of, store):
        w = words.astype(I32) ^ 0x88888
        for k in range(5):
            code = lax.shift_right_arithmetic(lax.shift_left(w, I32(28 - 4 * k)), I32(28))
            store(k, (code.astype(F32) * scale_of(k)).astype(BF16))

    def unpack_routed(b):
        local_gu[b].wait()

        def one(i, _):
            inner = i * 16
            for m in (0, 1):

                def scale_of(k):
                    return gu_scales[5 * b + k, pl.ds(m, 1), :]

                def store(k, value):
                    rows = pl.ds(al((5 * b + k) * 128 + inner, 16), 16)
                    weights[rows, m * HID : (m + 1) * HID] = value

                digits(rgu[m, pl.ds(al(128 * b + inner, 16), 16), :], scale_of, store)
            return 0

        lax.fori_loop(0, 8, one, 0)

    def routed_blocks(blocks):
        def one(j, _):
            rows = pl.ds(al(BLK * pick(j, blocks), 16), BLK)
            acc_r[...] += jnp.dot(
                xs_t[rows, :].T, weights[rows, :], preferred_element_type=F32
            )
            return 0

        lax.fori_loop(0, len(blocks), one, 0)

    def shared_shards(shards_in):
        def one(j, _):
            ee = pick(j, shards_in)

            def strip(i, _):
                s = 5 * ee + i
                b = s // 8
                inner = lax.rem(s, 8) * 16
                at = i * 16
                for k in range(5):
                    xperm[pl.ds(al(k * 80 + at, 16), 16), :] = tk_t[
                        pl.ds(al((5 * b + k) * 128 + inner, 16), 16), :
                    ]
                for m in (0, 1):

                    def scale_of(k):
                        return sgu_scales[5 * b + k, pl.ds(m, 1), :]

                    def store(k, value):
                        rows = pl.ds(al(k * 80 + at, 16), 16)
                        wshard[rows, m * HID : (m + 1) * HID] = value

                    digits(gu_all[m, pl.ds(al(s * 16, 16), 16), :], scale_of, store)
                return 0

            lax.fori_loop(0, 5, strip, 0)
            acc_s[...] += jnp.dot(xperm[...].T, wshard[...], preferred_element_type=F32)
            return 0

        lax.fori_loop(0, len(shards_in), one, 0)

    def activate(acc, target):
        g = acc[:, 0:HID]
        h = g / (1.0 + jnp.exp(-g)) * acc[:, HID : 2 * HID]
        target[...] = h.astype(BF16).T

    def down_blocks(words, lane, hid, target, blocks, then=None):
        def one(j, _):
            i = pick(j, blocks)

            def strip(q, _):
                rows = pl.ds(al(BLK * i + q * 80, 16), 80)

                def scale_of(k):
                    return scale_cols[rows, lane + k : lane + k + 1]

                def store(k, value):
                    wdown[pl.ds(al(q * 80, 16), 80), k * 128 : (k + 1) * 128] = value

                digits(words[rows, :], scale_of, store)
                return 0

            lax.fori_loop(0, 5, strip, 0)
            y = jnp.dot(wdown[...], hid[...], preferred_element_type=F32)
            target[pl.ds(al(BLK * i, 16), BLK), :] = y.astype(BF16)
            return 0

        lax.fori_loop(0, len(blocks), one, 0)

    local_tok.wait()
    local_ids.wait()
    expert_row = ids[...]
    onehot = (lax.broadcasted_iota(I32, (16, TOK), 0) == expert_row).astype(F32)
    upto = (
        lax.broadcasted_iota(I32, (TOK, TOK), 0) <= lax.broadcasted_iota(I32, (TOK, TOK), 1)
    ).astype(BF16)
    counted = jnp.dot(onehot.astype(BF16), upto, preferred_element_type=F32)
    rank = jnp.sum(counted * onehot, axis=0, keepdims=True) - 1.0
    slot = expert_row.astype(F32) * 16.0 + rank
    chosen = lax.broadcasted_iota(I32, (SLOTS, TOK), 0).astype(F32) == slot
    select[...] = chosen.astype(F32).astype(BF16)
    disp[...] = lax.dot_general(
        select[...], tk_t[own_rows, :], (((1,), (1,)), ((), ())), preferred_element_type=F32
    ).astype(BF16)
    local_sgu.wait()
    local_sdn.wait()
    local_gs.wait()

    def a2a(src, dst, k):
        def one(i, _):
            to = lax.rem(exp + i, 16)
            copy(
                src.at[pl.ds(al(16 * to, 16), 16), :],
                dst.at[pl.ds(al(16 * exp, 16), 16), :],
                asend.at[k],
                arecv.at[k],
                {"expert": to},
            ).start()
            return 0

        lax.fori_loop(1, 16, one, 0)
        mine = pl.ds(al(16 * exp, 16), 16)
        dst[mine, :] = src[mine, :]

    def a2a_wait(dst, k):
        ref = dst.at[pl.ds(0, 240), :]
        copy(ref, ref, asend.at[k], arecv.at[k], {"seq": other}).wait_recv()

    def a2a_end(src, k):
        ref = src.at[pl.ds(0, 240), :]
        copy(ref, ref, asend.at[k], arecv.at[k], {"seq": other}).wait_send()

    pl.semaphore_wait(barrier, 18)

    a2a(disp, disp_in, 0)
    toks.r0()
    gate.r0()
    up.r0()
    acc_r[...] = jnp.zeros(acc_r.shape, F32)
    acc_s[...] = jnp.zeros(acc_s.shape, F32)
    unpack_routed(0)
    unpack_routed(1)
    unpack_routed(2)
    toks.step(1)
    unpack_routed(3)
    unpack_routed(4)
    toks.step(2)
    unpack_routed(5)
    a2a_wait(disp_in, 0)
    xs_t[own_rows, :] = disp_in[...].T
    slots.r0()
    unpack_routed(6)
    toks.step(3)
    unpack_routed(7)
    toks.step(4)
    unpack_routed(8)
    unpack_routed(9)

    local_ds.wait()
    local_sds.wait()
    local_dn.wait()
    local_ss.wait()
    for k in range(5):
        scale_rows[k : k + 1, :] = dn_scales[k, :, :]
    scale_rows[8:13, :] = sdn_scales[...]

    def turn(j, _):
        at = pl.ds(al(j * 128, 128), 128)
        scale_cols[at, 0:16] = scale_rows[:, at].T
        rdn_t[at, :] = rdn[:, at].T
        return 0

    lax.fori_loop(0, 50, turn, 0)
    slots.step(1)
    gate.r1()
    up.r1()
    down_a.r0()
    down_b.r0()
    slots.sibling_wait(0)
    routed_blocks([block_of(core, 0), block_of(other, 0)])
    for dz in (0, 1, -1, 2, -2, 3, -3, 4):
        toks.sibling_wait(dz)
    shared_shards(gate.arrived(0))
    slots.step(2)
    routed_blocks([block_of(core, 1), block_of(core, -1)])
    shared_shards(gate.arrived(1))
    slots.step(3)
    slots.sibling_wait(1)
    slots.sibling_wait(-1)
    routed_blocks([block_of(c, dz) for c, dz in ((other, 1), (other, -1), (core, 2), (core, -2))])
    gate.r2()
    up.r2()
    slots.step(4)
    down_a.r1()
    down_b.r1()
    slots.sibling_wait(2)
    slots.sibling_wait(-2)
    routed_blocks([block_of(c, dz) for c, dz in ((other, 2), (other, -2), (core, 3), (core, -3))])
    slots.sibling_wait(3)
    slots.sibling_wait(-3)
    slots.sibling_wait(4)
    routed_blocks([block_of(c, dz) for c, dz in ((other, 3), (other, -3), (core, 4), (other, 4))])
    activate(acc_r, hid_r)

    def routed_down(offsets):
        blocks = []
        for dz in offsets:
            blocks += [block_of(other, dz), block_of(core, dz)]
        down_blocks(rdn_t, 0, hid_r, part_r, blocks)
        for dz in offsets:
            sum_r.to_sibling(lax.rem(z + dz + NZ, NZ))

    def routed_wait(offsets):
        for dz in offsets:
            sum_r.sibling_wait(lax.rem(z + dz + NZ, NZ))

    routed_down((4,))
    routed_down((3, -3))
    routed_wait((4,))
    sum_r.step(0)
    gate.r3()
    up.r3()
    routed_wait((3, -3))
    sum_r.step(1)
    down_a.r2()
    down_b.r2()
    routed_down((2, -2))
    shared_shards(gate.arrived(2)[0:2])
    routed_wait((2, -2))
    sum_r.step(2)
    gate.r4()
    up.r4()
    routed_down((1, -1))
    shared_shards(gate.arrived(2)[2:6])
    routed_wait((1, -1))
    sum_r.step(3)
    down_a.r3()
    down_b.r3()
    routed_down((0,))
    shared_shards(gate.arrived(3))
    routed_wait((0,))
    back[...] = sum_r.end().astype(BF16).T
    a2a(back, back_in, 1)
    shared_shards(gate.arrived(4))
    activate(acc_s, hid_s)
    down_a.r4()
    down_b.r4()

    def shared_down(blocks):
        down_blocks(dn_all, 8, hid_s, part_s, blocks)

    def shared_order(offsets):
        blocks = []
        for dz in offsets:
            blocks += [block_of(other, dz), block_of(core, dz)]
        shared_down(blocks)
        for dz in offsets:
            sum_s.to_sibling(lax.rem(z + dz + NZ, NZ))

    def shared_wait(offsets):
        for dz in offsets:
            sum_s.sibling_wait(lax.rem(z + dz + NZ, NZ))

    shared_order((4,))
    shared_order((3, -3))
    shared_wait((4,))
    sum_s.step(0)
    shared_wait((3, -3))
    sum_s.step(1)
    shared_order((2, -2))
    shared_wait((2, -2))
    sum_s.step(2)
    shared_order((1, -1))
    shared_wait((1, -1))
    sum_s.step(3)
    shared_order((0,))
    shared_wait((0,))
    a2a_wait(back_in, 1)
    local_gate.wait()
    routed = lax.dot_general(
        back_in[...], select[...], (((0,), (0,)), ((), ())), preferred_element_type=F32
    )
    out[...] = (sum_s.end() + gate_w[...] * routed).astype(BF16)

    a2a_end(disp, 0)
    a2a_end(back, 1)
    for cp in sent:
        cp.wait_send()


def shards(
    tokens,
    expert_ids,
    gate_weights,
    gate_up_codes,
    gate_up_scales,
    down_codes,
    down_scales,
    shared_gate_up_codes,
    shared_gate_up_scales,
    shared_down_codes,
    shared_down_scales,
):
    hbm = pl.BlockSpec(memory_space=pl.ANY)
    V = pltpu.VMEM
    S = pltpu.SemaphoreType.DMA
    return pl.pallas_call(
        kernel,
        out_shape=jax.ShapeDtypeStruct((BLK, TOK), BF16),
        in_specs=[hbm] * 11,
        out_specs=pl.BlockSpec(memory_space=pltpu.VMEM),
        scratch_shapes=[
            V((1, TOK), I32),
            V((1, TOK), F32),
            V((50, 2, HID), F32),
            V((5, 1, D), F32),
            V((50, 2, HID), F32),
            V((5, D), F32),
            V((16, D), F32),
            V((D, 16), F32),
            V((2, 1280, HID), F32),
            V((128, D), F32),
            V((D, 128), F32),
            V((2, 1280, HID), F32),
            V((D, 128), F32),
            V((D, 2 * HID), BF16),
            V((BLK, 2 * HID), BF16),
            V((BLK, HID), BF16),
            V((D, SLOTS), BF16),
            V((D, TOK), BF16),
            V((BLK, TOK), BF16),
            V((SLOTS, 2 * HID), F32),
            V((TOK, 2 * HID), F32),
            V((HID, SLOTS), BF16),
            V((HID, TOK), BF16),
            V((D, SLOTS), BF16),
            V((D, TOK), BF16),
            V((3200, SLOTS), BF16),
            V((3200, TOK), BF16),
            V((4, BLK, SLOTS), BF16),
            V((4, BLK, SLOTS), BF16),
            V((4, BLK, TOK), BF16),
            V((4, BLK, TOK), BF16),
            V((SLOTS, TOK), BF16),
            V((SLOTS, BLK), BF16),
            V((SLOTS, BLK), BF16),
            V((SLOTS, BLK), BF16),
            V((SLOTS, BLK), BF16),
            S((80,)),
            S((80,)),
            S((64,)),
            S((64,)),
            S((2,)),
            S((2,)),
            S((48,)),
            S((48,)),
            S((20,)),
        ],
        compiler_params=pltpu.CompilerParams(
            collective_id=0, has_side_effects=True, vmem_limit_bytes=64 * 1024 * 1024 - 65536
        ),
    )(
        tokens.T,
        expert_ids.reshape(1, TOK),
        gate_weights.reshape(1, TOK),
        gate_up_codes[0],
        jnp.transpose(gate_up_scales[0], (1, 0, 2)),
        down_codes[0],
        jnp.transpose(down_scales, (1, 0, 2)),
        shared_gate_up_codes,
        jnp.transpose(shared_gate_up_scales, (1, 0, 2)),
        shared_down_codes.T,
        shared_down_scales,
    ).T


def solution(mesh):
    placed = (
        P("expert", ("seq", "tensor")),
        P("expert"),
        P("expert"),
        P("expert", None, None, ("seq", "tensor")),
        P("expert", None, None, ("seq", "tensor")),
        P("expert", ("seq", "tensor"), None),
        P("expert", ("seq", "tensor"), None),
        P(None, "expert", ("seq", "tensor")),
        P(None, None, ("seq", "tensor")),
        P(("seq", "tensor"), "expert"),
        P(("seq", "tensor"), None),
    )
    return jax.shard_map(
        shards,
        mesh=mesh,
        in_specs=placed,
        out_specs=P("expert", ("seq", "tensor")),
        check_vma=False,
    )
```

time: 144 us -> 119 us (0.83)
  Pallas kernels: 133 us -> 117 us
  local copies, waits for them, and re-layouts: 10 us -> 1.54 us
    pallas_call x1, Pallas kernels: 133 us -> 117 us  [shards(): pl.pallas_call(kernel, out_shape=jax.ShapeDtypeStruct((BLK, TOK), BF16),...]
    unnamed x5 -> x1, local copies, waits for them, and re-layouts: 8.36 us -> 1.54 us
    pallas_call x1 -> x0, local copies, waits for them, and re-layouts: 1.65 us -> none  [shards(): pl.pallas_call(kernel, out_shape=jax.ShapeDtypeStruct((TOK, BLK), BF16),...]
where the time goes in v1:
time: 119 us
  Pallas kernels  117 us (98%)
  local copies, waits for them, and re-layouts  1.54 us (1%)
    pallas_call x1, Pallas kernels, shards(): pl.pallas_call(kernel, out_shape=jax.ShapeDtypeStruct((BLK, TOK), BF16),...  117 us

profile of v1, /device:TPU:1, one launch (start us, length us, event | category | flops | bytes accessed | tf_op | source)
XLA Modules:
  0.0 118.9 jit_solution(7598808982751717292)
XLA Ops:
  0.0 117.3 %shard_map.109 = bf16[400,128]{1,0:T(8,128)(2,1)} custom-call(bf16[400,128]{1,0:T(8,128)(2,1)} %bitcast.19, s32[1,128]{1,0:T(1,128)} %bitcast.20, f32[1,128]{1,0:T(1,128)} %bitcast.21, f32[2,1280,640]{2,1,0:T(8,128)} %bitcast.12, f32[50,2,640]{2,1,0:T(2,128)} %bitcast.15, f32[128,6400]{1,0:T(8,128)} %bitcast.13, f32[5,1,6400]{2,1,0:T(1,128)} %bitcast.18, ...), custom_call_target="tpu_custom_call" | custom-call | tf_op jit(solution)/shard_map/pallas_call | solution.py:689
  117.3 1.5 %copy.13 = bf16[128,400]{0,1:T(8,128)(2,1)} copy(bf16[128,400]{0,1:T(8,128)(2,1)} %bitcast.14) | data formatting | bytes 204800

commit v2 on v1

--- a/solution.py
+++ b/solution.py
@@ -49,16 +49,16 @@
     dn_scales,
     sgu_scales,
     sdn_scales,
-    scale_rows,
-    scale_cols,
+    scale_blocks,
     rgu,
     rdn,
-    rdn_t,
     gu_all,
     dn_all,
     weights,
     wshard,
-    wdown,
+    wchunk,
+    wblock,
+    turned,
     xs_t,
     tk_t,
     xperm,
@@ -270,23 +270,19 @@
                 k = self.base + 16 + 2 * (dz % NZ) + part
                 copy(ref, ref, zsend.at[k], zrecv.at[k], {"seq": other}).wait_recv()
 
-        def r0(self):
-            for part in (0, 1):
-                self.ring(True, 0, part)
-                self.ring(False, 0, part)
-            for part in (0, 1):
-                self.sibling(0, part)
-
-        def step(self, r):
-            for part in (0, 1):
-                for up_way in (True, False):
-                    long_way = (part == 0) == up_way
-                    if r == 4 and not long_way:
-                        continue
-                    self.ring_wait(up_way, r, part)
-                    if r <= (3 if long_way else 2):
-                        self.ring(up_way, r, part)
-                    self.sibling(-r if up_way else r, part)
+        def start(self, long_way):
+            part = 0 if long_way else 1
+            self.ring(True, 0, part)
+            self.ring(False, 0, 1 - part)
+            self.sibling(0, part)
+
+        def step(self, r, long_way):
+            for up_way in (True, False):
+                part = 0 if long_way == up_way else 1
+                self.ring_wait(up_way, r, part)
+                if r <= (3 if long_way else 2):
+                    self.ring(up_way, r, part)
+                self.sibling(-r if up_way else r, part)
 
     slots = Gather(xs_t, 0)
     toks = Gather(tk_t, 1)
@@ -297,20 +293,18 @@
             self.part, self.sib = part, sib
             self.recv = (precv, mrecv)
 
-        def to_sibling(self, d):
-            rows = pl.ds(al(BLK * (NZ * other + d), 16), BLK)
-            k = self.base + d
-            push(
-                self.part.at[rows, :],
-                self.sib.at[pl.ds(al(BLK * d, 16), BLK), :],
-                rsend.at[k],
-                rrecv.at[k],
+        def sibling_copy(self, at, size, k):
+            return copy(
+                self.part.at[pl.ds(al(3200 * other + at, 16), size), :],
+                self.sib.at[pl.ds(al(at, 16), size), :],
+                rsend.at[self.base + k],
+                rrecv.at[self.base + k],
                 {"seq": other},
             )
 
-        def sibling_wait(self, d):
-            ref = self.sib.at[pl.ds(al(BLK * d, 16), BLK), :]
-            k = self.base + d
+        def sibling_wait(self, at, size, k):
+            ref = self.sib.at[pl.ds(al(at, 16), size), :]
+            k = self.base + k
             copy(ref, ref, rsend.at[k], rrecv.at[k], {"seq": other}).wait_recv()
 
         def pair(self, d, part):
@@ -346,21 +340,13 @@
                 {"tensor": zplus if way == 0 else zminus},
             )
 
-        def step(self, s):
-            if s == 0:
-                self.message(0, 0, 0)
-                self.message(1, 0, 1)
-                return
-            if s == 1:
-                self.message(0, 1, 1)
-                self.message(1, 1, 0)
-                self.message(0, 1, 0)
-                self.message(1, 1, 1)
-                return
-            for part in (0, 1):
-                self.message(part, s, 1 - part)
-            for part in (0, 1):
-                self.message(part, s, part)
+        def long_step(self, s):
+            self.message(0, s, 0)
+            self.message(1, s, 1)
+
+        def short_step(self, s):
+            self.message(0, s, 1)
+            self.message(1, s, 0)
 
         def end(self):
             for way in (0, 1):
@@ -444,27 +430,46 @@
     def activate(acc, target):
         g = acc[:, 0:HID]
         h = g / (1.0 + jnp.exp(-g)) * acc[:, HID : 2 * HID]
-        target[...] = h.astype(BF16).T
-
-    def down_blocks(words, lane, hid, target, blocks, then=None):
+        target[...] = h.astype(BF16)
+
+    def unpack_down(words, rows_of_scales, target):
+        def strip(q, _):
+            at = pl.ds(al(q * 16, 16), 16)
+
+            def store(k, value):
+                target[pl.ds(al(k * 128 + q * 16, 16), 16), :] = value
+
+            digits(words(at), rows_of_scales, store)
+            return 0
+
+        lax.fori_loop(0, 8, strip, 0)
+
+    def routed_chunks(chunks):
         def one(j, _):
-            i = pick(j, blocks)
-
-            def strip(q, _):
-                rows = pl.ds(al(BLK * i + q * 80, 16), 80)
-
-                def scale_of(k):
-                    return scale_cols[rows, lane + k : lane + k + 1]
-
-                def store(k, value):
-                    wdown[pl.ds(al(q * 80, 16), 80), k * 128 : (k + 1) * 128] = value
-
-                digits(words[rows, :], scale_of, store)
-                return 0
-
-            lax.fori_loop(0, 5, strip, 0)
-            y = jnp.dot(wdown[...], hid[...], preferred_element_type=F32)
-            target[pl.ds(al(BLK * i, 16), BLK), :] = y.astype(BF16)
+            cols = pl.ds(al(HID * pick(j, chunks), 128), HID)
+            unpack_down(lambda at: rdn[at, cols], lambda k: dn_scales[k, :, cols], wchunk)
+            y = jnp.dot(hid_r[...], wchunk[...], preferred_element_type=F32)
+            part_r[cols, :] = y.astype(BF16).T
+            return 0
+
+        lax.fori_loop(0, len(chunks), one, 0)
+
+    def shared_down(blocks):
+        def one(j, _):
+            ee = pick(j, blocks)
+            rows = pl.ds(al(BLK * ee, 16), BLK)
+            turned[...] = dn_all[rows, :].T
+            unpack_down(
+                lambda at: turned[at, :], lambda k: scale_blocks[ee, pl.ds(k, 1), :], wblock
+            )
+            y = jnp.dot(hid_s[...], wblock[...], preferred_element_type=F32)
+            part_s[rows, :] = y.astype(BF16).T
+
+            @pl.when(ee // NZ == other)
+            def _():
+                d = lax.rem(ee, NZ)
+                sum_s.sibling_copy(BLK * d, BLK, d).start()
+
             return 0
 
         lax.fori_loop(0, len(blocks), one, 0)
@@ -512,150 +517,144 @@
         ref = src.at[pl.ds(0, 240), :]
         copy(ref, ref, asend.at[k], arecv.at[k], {"seq": other}).wait_send()
 
-    pl.semaphore_wait(barrier, 18)
-
-    a2a(disp, disp_in, 0)
-    toks.r0()
-    gate.r0()
-    up.r0()
     acc_r[...] = jnp.zeros(acc_r.shape, F32)
     acc_s[...] = jnp.zeros(acc_s.shape, F32)
     unpack_routed(0)
     unpack_routed(1)
+    pl.semaphore_wait(barrier, 18)
+
+    a2a(disp, disp_in, 0)
+    toks.start(True)
+    gate.r0()
+    up.r0()
     unpack_routed(2)
-    toks.step(1)
+    toks.start(False)
     unpack_routed(3)
     unpack_routed(4)
-    toks.step(2)
+    toks.step(1, True)
     unpack_routed(5)
+    toks.step(1, False)
+    unpack_routed(6)
+    toks.step(2, True)
     a2a_wait(disp_in, 0)
     xs_t[own_rows, :] = disp_in[...].T
-    slots.r0()
-    unpack_routed(6)
-    toks.step(3)
+    slots.start(True)
+    toks.step(2, False)
     unpack_routed(7)
-    toks.step(4)
     unpack_routed(8)
+    toks.step(3, True)
+    slots.start(False)
     unpack_routed(9)
-
-    local_ds.wait()
+    toks.step(3, False)
+    toks.step(4, True)
+    local_ss.wait()
     local_sds.wait()
-    local_dn.wait()
-    local_ss.wait()
-    for k in range(5):
-        scale_rows[k : k + 1, :] = dn_scales[k, :, :]
-    scale_rows[8:13, :] = sdn_scales[...]
-
-    def turn(j, _):
-        at = pl.ds(al(j * 128, 128), 128)
-        scale_cols[at, 0:16] = scale_rows[:, at].T
-        rdn_t[at, :] = rdn[:, at].T
-        return 0
-
-    lax.fori_loop(0, 50, turn, 0)
-    slots.step(1)
+    for i in range(16):
+        scale_blocks[i, 0:5, :] = sdn_scales[:, BLK * i : BLK * (i + 1)]
     gate.r1()
     up.r1()
     down_a.r0()
     down_b.r0()
-    slots.sibling_wait(0)
-    routed_blocks([block_of(core, 0), block_of(other, 0)])
+    slots.step(1, True)
     for dz in (0, 1, -1, 2, -2, 3, -3, 4):
         toks.sibling_wait(dz)
     shared_shards(gate.arrived(0))
-    slots.step(2)
+    slots.sibling_wait(0)
+    routed_blocks([block_of(core, 0), block_of(other, 0)])
+    slots.step(1, False)
     routed_blocks([block_of(core, 1), block_of(core, -1)])
-    shared_shards(gate.arrived(1))
-    slots.step(3)
+    shared_shards(gate.arrived(1)[0:1])
+    slots.step(2, True)
     slots.sibling_wait(1)
     slots.sibling_wait(-1)
-    routed_blocks([block_of(c, dz) for c, dz in ((other, 1), (other, -1), (core, 2), (core, -2))])
+    routed_blocks([block_of(other, 1), block_of(other, -1)])
+    shared_shards(gate.arrived(1)[1:2])
+    slots.step(2, False)
+    routed_blocks([block_of(core, 2), block_of(core, -2)])
+    shared_shards(gate.arrived(1)[2:3])
+    slots.step(3, True)
+    slots.sibling_wait(2)
+    slots.sibling_wait(-2)
+    routed_blocks([block_of(other, 2), block_of(other, -2)])
+    shared_shards(gate.arrived(1)[3:4])
+    slots.step(3, False)
+    routed_blocks([block_of(core, 3), block_of(core, -3)])
     gate.r2()
     up.r2()
-    slots.step(4)
+    slots.step(4, True)
     down_a.r1()
     down_b.r1()
-    slots.sibling_wait(2)
-    slots.sibling_wait(-2)
-    routed_blocks([block_of(c, dz) for c, dz in ((other, 2), (other, -2), (core, 3), (core, -3))])
     slots.sibling_wait(3)
     slots.sibling_wait(-3)
     slots.sibling_wait(4)
     routed_blocks([block_of(c, dz) for c, dz in ((other, 3), (other, -3), (core, 4), (other, 4))])
     activate(acc_r, hid_r)
 
+    local_ds.wait()
+    local_dn.wait()
+    first = BLK * lax.rem(z + 4, NZ) // HID
+
     def routed_down(offsets):
-        blocks = []
-        for dz in offsets:
-            blocks += [block_of(other, dz), block_of(core, dz)]
-        down_blocks(rdn_t, 0, hid_r, part_r, blocks)
-        for dz in offsets:
-            sum_r.to_sibling(lax.rem(z + dz + NZ, NZ))
-
-    def routed_wait(offsets):
-        for dz in offsets:
-            sum_r.sibling_wait(lax.rem(z + dz + NZ, NZ))
-
-    routed_down((4,))
-    routed_down((3, -3))
-    routed_wait((4,))
-    sum_r.step(0)
+        qs = [lax.rem(first + q, 5) for q in offsets]
+        routed_chunks([5 * other + q for q in qs])
+        for q in qs:
+            cp = sum_r.sibling_copy(HID * q, HID, q)
+            cp.start()
+            sent.append(cp)
+        routed_chunks([5 * core + q for q in qs])
+        for q in qs:
+            sum_r.sibling_wait(HID * q, HID, q)
+
+    routed_down((0, 1))
+    sum_r.long_step(0)
+    routed_down((4, 2))
+    sum_r.short_step(1)
     gate.r3()
     up.r3()
-    routed_wait((3, -3))
-    sum_r.step(1)
+    sum_r.long_step(1)
     down_a.r2()
     down_b.r2()
-    routed_down((2, -2))
-    shared_shards(gate.arrived(2)[0:2])
-    routed_wait((2, -2))
-    sum_r.step(2)
+    routed_down((3,))
+    sum_r.short_step(2)
+    shared_shards(gate.arrived(2)[0:3])
+    sum_r.long_step(2)
     gate.r4()
     up.r4()
-    routed_down((1, -1))
-    shared_shards(gate.arrived(2)[2:6])
-    routed_wait((1, -1))
-    sum_r.step(3)
+    shared_shards(gate.arrived(2)[3:6])
+    sum_r.short_step(3)
     down_a.r3()
     down_b.r3()
-    routed_down((0,))
-    shared_shards(gate.arrived(3))
-    routed_wait((0,))
+    shared_shards(gate.arrived(3)[0:2])
+    sum_r.long_step(3)
+    shared_shards(gate.arrived(3)[2:4])
+    shared_shards(gate.arrived(4))
+    activate(acc_s, hid_s)
+    shared_down(gate.arrived(0))
     back[...] = sum_r.end().astype(BF16).T
     a2a(back, back_in, 1)
-    shared_shards(gate.arrived(4))
-    activate(acc_s, hid_s)
+    shared_down(gate.arrived(1))
+    shared_down(gate.arrived(2))
+    shared_down(gate.arrived(3))
     down_a.r4()
     down_b.r4()
-
-    def shared_down(blocks):
-        down_blocks(dn_all, 8, hid_s, part_s, blocks)
-
-    def shared_order(offsets):
-        blocks = []
-        for dz in offsets:
-            blocks += [block_of(other, dz), block_of(core, dz)]
-        shared_down(blocks)
-        for dz in offsets:
-            sum_s.to_sibling(lax.rem(z + dz + NZ, NZ))
+    shared_down(gate.arrived(4))
 
     def shared_wait(offsets):
         for dz in offsets:
-            sum_s.sibling_wait(lax.rem(z + dz + NZ, NZ))
-
-    shared_order((4,))
-    shared_order((3, -3))
+            d = lax.rem(z + dz + NZ, NZ)
+            sum_s.sibling_wait(BLK * d, BLK, d)
+
     shared_wait((4,))
-    sum_s.step(0)
+    sum_s.long_step(0)
     shared_wait((3, -3))
-    sum_s.step(1)
-    shared_order((2, -2))
+    sum_s.short_step(1)
+    sum_s.long_step(1)
     shared_wait((2, -2))
-    sum_s.step(2)
-    shared_order((1, -1))
+    sum_s.short_step(2)
+    sum_s.long_step(2)
     shared_wait((1, -1))
-    sum_s.step(3)
-    shared_order((0,))
+    sum_s.short_step(3)
+    sum_s.long_step(3)
     shared_wait((0,))
     a2a_wait(back_in, 1)
     local_gate.wait()
@@ -664,6 +663,8 @@
     )
     out[...] = (sum_s.end() + gate_w[...] * routed).astype(BF16)
 
+    for d in range(NZ):
+        sum_s.sibling_copy(BLK * d, BLK, d).wait_send()
     a2a_end(disp, 0)
     a2a_end(back, 1)
     for cp in sent:
@@ -698,23 +699,23 @@
             V((5, 1, D), F32),
             V((50, 2, HID), F32),
             V((5, D), F32),
-            V((16, D), F32),
-            V((D, 16), F32),
+            V((16, 8, BLK), F32),
             V((2, 1280, HID), F32),
             V((128, D), F32),
-            V((D, 128), F32),
             V((2, 1280, HID), F32),
             V((D, 128), F32),
             V((D, 2 * HID), BF16),
             V((BLK, 2 * HID), BF16),
-            V((BLK, HID), BF16),
+            V((HID, HID), BF16),
+            V((HID, BLK), BF16),
+            V((128, BLK), F32),
             V((D, SLOTS), BF16),
             V((D, TOK), BF16),
             V((BLK, TOK), BF16),
             V((SLOTS, 2 * HID), F32),
             V((TOK, 2 * HID), F32),
-            V((HID, SLOTS), BF16),
-            V((HID, TOK), BF16),
+            V((SLOTS, HID), BF16),
+            V((TOK, HID), BF16),
             V((D, SLOTS), BF16),
             V((D, TOK), BF16),
             V((3200, SLOTS), BF16),

time: 119 us -> 105 us (0.88)
  Pallas kernels: 117 us -> 103 us
    pallas_call x1, Pallas kernels: 117 us -> 103 us  [shards(): pl.pallas_call(kernel, out_shape=jax.ShapeDtypeStruct((BLK, TOK), BF16),...]
where the time goes in v2:
time: 105 us
  Pallas kernels  103 us (98%)
  local copies, waits for them, and re-layouts  1.54 us (1%)
    pallas_call x1, Pallas kernels, shards(): pl.pallas_call(kernel, out_shape=jax.ShapeDtypeStruct((BLK, TOK), BF16),...  103 us

profile of v2, /device:TPU:1, one launch (start us, length us, event | category | flops | bytes accessed | tf_op | source)
XLA Modules:
  0.0 104.9 jit_solution(17982014974339736654)
XLA Ops:
  0.0 103.4 %shard_map.109 = bf16[400,128]{1,0:T(8,128)(2,1)} custom-call(bf16[400,128]{1,0:T(8,128)(2,1)} %bitcast.19, s32[1,128]{1,0:T(1,128)} %bitcast.20, f32[1,128]{1,0:T(1,128)} %bitcast.21, f32[2,1280,640]{2,1,0:T(8,128)} %bitcast.12, f32[50,2,640]{2,1,0:T(2,128)} %bitcast.15, f32[128,6400]{1,0:T(8,128)} %bitcast.13, f32[5,1,6400]{2,1,0:T(1,128)} %bitcast.18, ...), custom_call_target="tpu_custom_call" | custom-call | tf_op jit(solution)/shard_map/pallas_call | solution.py:690
  103.4 1.5 %copy.13 = bf16[128,400]{0,1:T(8,128)(2,1)} copy(bf16[128,400]{0,1:T(8,128)(2,1)} %bitcast.14) | data formatting | bytes 204800

commit v3 on v2

--- a/solution.py
+++ b/solution.py
@@ -464,12 +464,6 @@
             )
             y = jnp.dot(hid_s[...], wblock[...], preferred_element_type=F32)
             part_s[rows, :] = y.astype(BF16).T
-
-            @pl.when(ee // NZ == other)
-            def _():
-                d = lax.rem(ee, NZ)
-                sum_s.sibling_copy(BLK * d, BLK, d).start()
-
             return 0
 
         lax.fori_loop(0, len(blocks), one, 0)
@@ -530,60 +524,60 @@
     unpack_routed(2)
     toks.start(False)
     unpack_routed(3)
+    down_a.r0()
+    down_b.r0()
     unpack_routed(4)
     toks.step(1, True)
     unpack_routed(5)
     toks.step(1, False)
     unpack_routed(6)
-    toks.step(2, True)
     a2a_wait(disp_in, 0)
     xs_t[own_rows, :] = disp_in[...].T
     slots.start(True)
+    toks.step(2, True)
+    unpack_routed(7)
     toks.step(2, False)
-    unpack_routed(7)
     unpack_routed(8)
-    toks.step(3, True)
     slots.start(False)
     unpack_routed(9)
-    toks.step(3, False)
-    toks.step(4, True)
+    toks.step(3, True)
     local_ss.wait()
     local_sds.wait()
     for i in range(16):
         scale_blocks[i, 0:5, :] = sdn_scales[:, BLK * i : BLK * (i + 1)]
+    down_a.r1()
+    down_b.r1()
+    toks.step(3, False)
     gate.r1()
     up.r1()
-    down_a.r0()
-    down_b.r0()
     slots.step(1, True)
-    for dz in (0, 1, -1, 2, -2, 3, -3, 4):
-        toks.sibling_wait(dz)
-    shared_shards(gate.arrived(0))
+    toks.step(4, True)
     slots.sibling_wait(0)
     routed_blocks([block_of(core, 0), block_of(other, 0)])
     slots.step(1, False)
     routed_blocks([block_of(core, 1), block_of(core, -1)])
-    shared_shards(gate.arrived(1)[0:1])
+    for dz in (0, 1, -1, 2, -2, 3, -3, 4):
+        toks.sibling_wait(dz)
+    shared_shards(gate.arrived(0))
     slots.step(2, True)
     slots.sibling_wait(1)
     slots.sibling_wait(-1)
     routed_blocks([block_of(other, 1), block_of(other, -1)])
-    shared_shards(gate.arrived(1)[1:2])
+    shared_shards(gate.arrived(1)[0:1])
     slots.step(2, False)
     routed_blocks([block_of(core, 2), block_of(core, -2)])
-    shared_shards(gate.arrived(1)[2:3])
+    shared_shards(gate.arrived(1)[1:2])
     slots.step(3, True)
     slots.sibling_wait(2)
     slots.sibling_wait(-2)
     routed_blocks([block_of(other, 2), block_of(other, -2)])
-    shared_shards(gate.arrived(1)[3:4])
+    shared_shards(gate.arrived(1)[2:3])
     slots.step(3, False)
     routed_blocks([block_of(core, 3), block_of(core, -3)])
-    gate.r2()
-    up.r2()
+    shared_shards(gate.arrived(1)[3:4])
+    down_a.r2()
+    down_b.r2()
     slots.step(4, True)
-    down_a.r1()
-    down_b.r1()
     slots.sibling_wait(3)
     slots.sibling_wait(-3)
     slots.sibling_wait(4)
@@ -607,55 +601,57 @@
 
     routed_down((0, 1))
     sum_r.long_step(0)
+    gate.r2()
+    up.r2()
     routed_down((4, 2))
     sum_r.short_step(1)
+    sum_r.long_step(1)
+    routed_down((3,))
+    down_a.r3()
+    down_b.r3()
+    shared_shards(gate.arrived(2)[0:2])
+    sum_r.short_step(2)
+    shared_shards(gate.arrived(2)[2:3])
+    sum_r.long_step(2)
+    shared_shards(gate.arrived(2)[3:6])
     gate.r3()
     up.r3()
-    sum_r.long_step(1)
-    down_a.r2()
-    down_b.r2()
-    routed_down((3,))
-    sum_r.short_step(2)
-    shared_shards(gate.arrived(2)[0:3])
-    sum_r.long_step(2)
+    sum_r.short_step(3)
+    shared_shards(gate.arrived(3)[0:1])
+    sum_r.long_step(3)
+    shared_shards(gate.arrived(3)[1:4])
+    down_a.r4()
+    down_b.r4()
     gate.r4()
     up.r4()
-    shared_shards(gate.arrived(2)[3:6])
-    sum_r.short_step(3)
-    down_a.r3()
-    down_b.r3()
-    shared_shards(gate.arrived(3)[0:2])
-    sum_r.long_step(3)
-    shared_shards(gate.arrived(3)[2:4])
     shared_shards(gate.arrived(4))
     activate(acc_s, hid_s)
-    shared_down(gate.arrived(0))
+
+    def shared_order(offsets):
+        ds = [lax.rem(z + dz + NZ, NZ) for dz in offsets]
+        shared_down([NZ * other + d for d in ds])
+        for d in ds:
+            cp = sum_s.sibling_copy(BLK * d, BLK, d)
+            cp.start()
+            sent.append(cp)
+        shared_down([NZ * core + d for d in ds])
+        for d in ds:
+            sum_s.sibling_wait(BLK * d, BLK, d)
+
+    shared_order((4,))
+    sum_s.long_step(0)
     back[...] = sum_r.end().astype(BF16).T
     a2a(back, back_in, 1)
-    shared_down(gate.arrived(1))
-    shared_down(gate.arrived(2))
-    shared_down(gate.arrived(3))
-    down_a.r4()
-    down_b.r4()
-    shared_down(gate.arrived(4))
-
-    def shared_wait(offsets):
-        for dz in offsets:
-            d = lax.rem(z + dz + NZ, NZ)
-            sum_s.sibling_wait(BLK * d, BLK, d)
-
-    shared_wait((4,))
-    sum_s.long_step(0)
-    shared_wait((3, -3))
+    shared_order((3, -3))
     sum_s.short_step(1)
     sum_s.long_step(1)
-    shared_wait((2, -2))
+    shared_order((2, -2))
     sum_s.short_step(2)
     sum_s.long_step(2)
-    shared_wait((1, -1))
+    shared_order((1, -1))
     sum_s.short_step(3)
     sum_s.long_step(3)
-    shared_wait((0,))
+    shared_order((0,))
     a2a_wait(back_in, 1)
     local_gate.wait()
     routed = lax.dot_general(
@@ -663,8 +659,6 @@
     )
     out[...] = (sum_s.end() + gate_w[...] * routed).astype(BF16)
 
-    for d in range(NZ):
-        sum_s.sibling_copy(BLK * d, BLK, d).wait_send()
     a2a_end(disp, 0)
     a2a_end(back, 1)
     for cp in sent:

time: 105 us -> 93.9 us (0.89)
  Pallas kernels: 103 us -> 92.2 us
    pallas_call x1, Pallas kernels: 103 us -> 92.2 us  [shards(): pl.pallas_call(kernel, out_shape=jax.ShapeDtypeStruct((BLK, TOK), BF16),...]
where the time goes in v3:
time: 93.9 us; the launch traced here: 93.8 us
  Pallas kernels  92.2 us (98%)
  local copies, waits for them, and re-layouts  1.54 us (2%)
    pallas_call x1, Pallas kernels, shards(): pl.pallas_call(kernel, out_shape=jax.ShapeDtypeStruct((BLK, TOK), BF16),...  92.2 us

profile of v3, /device:TPU:1, one launch (start us, length us, event | category | flops | bytes accessed | tf_op | source)
XLA Modules:
  0.0 93.8 jit_solution(1597122785148868631)
XLA Ops:
  0.0 92.2 %shard_map.109 = bf16[400,128]{1,0:T(8,128)(2,1)} custom-call(bf16[400,128]{1,0:T(8,128)(2,1)} %bitcast.19, s32[1,128]{1,0:T(1,128)} %bitcast.20, f32[1,128]{1,0:T(1,128)} %bitcast.21, f32[2,1280,640]{2,1,0:T(8,128)} %bitcast.12, f32[50,2,640]{2,1,0:T(2,128)} %bitcast.15, f32[128,6400]{1,0:T(8,128)} %bitcast.13, f32[5,1,6400]{2,1,0:T(1,128)} %bitcast.18, ...), custom_call_target="tpu_custom_call" | custom-call | tf_op jit(solution)/shard_map/pallas_call | solution.py:684
  92.2 1.5 %copy.13 = bf16[128,400]{0,1:T(8,128)(2,1)} copy(bf16[128,400]{0,1:T(8,128)(2,1)} %bitcast.14) | data formatting | bytes 204800

commit v4 on v3

--- a/solution.py
+++ b/solution.py
@@ -49,15 +49,15 @@
     dn_scales,
     sgu_scales,
     sdn_scales,
-    scale_blocks,
     rgu,
     rdn,
-    gu_all,
-    dn_all,
+    own_gu,
+    own_dn,
+    packed,
+    turn_in,
     weights,
     wshard,
     wchunk,
-    wblock,
     turned,
     xs_t,
     tk_t,
@@ -117,12 +117,11 @@
         return cp
 
     own_rows = pl.ds(al(3200 * core + BLK * z, 16), BLK)
-    dn_rows = pl.ds(al(BLK * exp, 16), BLK)
     local_tok = load(tokens, tk_t.at[own_rows, :], 0)
     local_ids = load(ids_in, ids, 1)
     local_gate = load(gate_in, gate_w, 2)
-    local_sgu = load(sgu_codes, gu_all.at[:, pl.ds(al(80 * exp, 8), 80), :], 3)
-    local_sdn = load(sdn_codes, dn_all.at[dn_rows, :], 4)
+    local_sgu = load(sgu_codes, own_gu, 3)
+    local_sdn = load(sdn_codes, own_dn, 4)
     local_gs = load(gu_scales_in, gu_scales, 5)
     local_gu = []
     for b in range(10):
@@ -150,13 +149,26 @@
         cp.start()
         sent.append(cp)
 
+    def drain(keep):
+        while len(sent) > keep:
+            sent.pop(0).wait_send()
+
+    def pack_own():
+        for r in range(10):
+            for c in range(5):
+                rows, cols = pl.ds(8 * r, 8), pl.ds(128 * c, 128)
+                g = own_gu[0, rows, cols].astype(I32)
+                u = own_gu[1, rows, cols].astype(I32)
+                d = own_dn[pl.ds(8 * (5 * r + c), 8), :].astype(I32)
+                low = (g | lax.shift_left(u, I32(20))) ^ I32(-0x77777778)
+                high = (lax.shift_right_logical(u, I32(12)) | lax.shift_left(d, I32(8))) ^ I32(0x08888888)
+                at = pl.ds(al(80 * exp + 8 * r, 8), 8)
+                packed[0, at, cols] = low
+                packed[1, at, cols] = high
+
     def region(piece, ee, half):
-        if piece < 2:
-            off, size = ((0, 80), (0, 40), (40, 40))[half]
-            return gu_all.at[piece, pl.ds(al(80 * ee + off, 8), size), :]
-        base = 200 * (piece - 2)
-        off, size = ((0, 200), (0, 104), (104, 96))[half]
-        return dn_all.at[pl.ds(al(400 * ee + (base + off), 8), size), :]
+        off, size = ((0, 80), (0, 40), (40, 40))[half]
+        return packed.at[piece, pl.ds(al(80 * ee + off, 8), size), :]
 
     class Piece:
         def __init__(self, piece):
@@ -234,7 +246,7 @@
             )[r]
             return [self.block(da, db) for da, db in places]
 
-    gate, up, down_a, down_b = (Piece(i) for i in range(4))
+    low, high = Piece(0), Piece(1)
 
     def block_of(c, dz):
         return NZ * c + lax.rem(z + dz + NZ, NZ)
@@ -250,31 +262,31 @@
 
         def ring(self, up_way, r, part):
             ref = self.rows(core, -r if up_way else r, part)
-            k = self.base + (0 if up_way else 8) + 2 * r + part
+            k = self.base + (0 if up_way else 8) + 2 * r + part % 2
             to = zplus if up_way else zminus
             push(ref, ref, zsend.at[k], zrecv.at[k], {"tensor": to})
 
-        def sibling(self, dz, part):
-            ref = self.rows(core, dz, part)
-            k = self.base + 16 + 2 * (dz % NZ) + part
+        def sibling(self, dz):
+            ref = self.rows(core, dz, 2)
+            k = self.base + 16 + dz % NZ
             push(ref, ref, zsend.at[k], zrecv.at[k], {"seq": other})
 
         def ring_wait(self, up_way, r, part):
             ref = self.rows(core, -r if up_way else r, part)
-            k = self.base + (0 if up_way else 8) + 2 * (r - 1) + part
+            k = self.base + (0 if up_way else 8) + 2 * (r - 1) + part % 2
             copy(ref, ref, zsend.at[k], zrecv.at[k], {"tensor": zplus}).wait_recv()
 
         def sibling_wait(self, dz):
-            for part in (0, 1):
-                ref = self.rows(other, dz, part)
-                k = self.base + 16 + 2 * (dz % NZ) + part
-                copy(ref, ref, zsend.at[k], zrecv.at[k], {"seq": other}).wait_recv()
+            ref = self.rows(other, dz, 2)
+            k = self.base + 16 + dz % NZ
+            copy(ref, ref, zsend.at[k], zrecv.at[k], {"seq": other}).wait_recv()
 
         def start(self, long_way):
             part = 0 if long_way else 1
             self.ring(True, 0, part)
             self.ring(False, 0, 1 - part)
-            self.sibling(0, part)
+            if long_way:
+                self.sibling(0)
 
         def step(self, r, long_way):
             for up_way in (True, False):
@@ -282,7 +294,26 @@
                 self.ring_wait(up_way, r, part)
                 if r <= (3 if long_way else 2):
                     self.ring(up_way, r, part)
-                self.sibling(-r if up_way else r, part)
+                if not long_way:
+                    self.sibling(-r if up_way else r)
+            if r == 4:
+                self.sibling(4)
+
+        def start_whole(self):
+            self.ring(True, 0, 2)
+            self.ring(False, 0, 2)
+            self.sibling(0)
+
+        def step_whole(self, r):
+            self.ring_wait(True, r, 2)
+            if r <= 3:
+                self.ring(True, r, 2)
+            self.sibling(-r)
+            if r <= 3:
+                self.ring_wait(False, r, 2)
+                if r <= 2:
+                    self.ring(False, r, 2)
+                self.sibling(r)
 
     slots = Gather(xs_t, 0)
     toks = Gather(tk_t, 1)
@@ -361,11 +392,14 @@
     sum_r = Scatter(0, part_r, sib_r, precv_r, mrecv_r)
     sum_s = Scatter(1, part_s, sib_s, precv_s, mrecv_s)
 
+    def scaled(w, bit, scale):
+        code = lax.shift_right_arithmetic(lax.shift_left(w, I32(28 - bit)), I32(28))
+        return (code.astype(F32) * scale).astype(BF16)
+
     def digits(words, scale_of, store):
         w = words.astype(I32) ^ 0x88888
         for k in range(5):
-            code = lax.shift_right_arithmetic(lax.shift_left(w, I32(28 - 4 * k)), I32(28))
-            store(k, (code.astype(F32) * scale_of(k)).astype(BF16))
+            store(k, scaled(w, 4 * k, scale_of(k)))
 
     def unpack_routed(b):
         local_gu[b].wait()
@@ -396,36 +430,43 @@
 
         lax.fori_loop(0, len(blocks), one, 0)
 
-    def shared_shards(shards_in):
+    def shared_shards(shards_in, place):
         def one(j, _):
             ee = pick(j, shards_in)
+            first_row = BLK * (place + j)
 
             def strip(i, _):
                 s = 5 * ee + i
                 b = s // 8
                 inner = lax.rem(s, 8) * 16
-                at = i * 16
+                at = first_row + i * 16
                 for k in range(5):
                     xperm[pl.ds(al(k * 80 + at, 16), 16), :] = tk_t[
                         pl.ds(al((5 * b + k) * 128 + inner, 16), 16), :
                     ]
-                for m in (0, 1):
-
-                    def scale_of(k):
-                        return sgu_scales[5 * b + k, pl.ds(m, 1), :]
-
-                    def store(k, value):
-                        rows = pl.ds(al(k * 80 + at, 16), 16)
-                        wshard[rows, m * HID : (m + 1) * HID] = value
-
-                    digits(gu_all[m, pl.ds(al(s * 16, 16), 16), :], scale_of, store)
+                words = pl.ds(al(s * 16, 16), 16)
+                w0 = packed[0, words, :]
+                w1 = packed[1, words, :]
+                for k in range(5):
+                    rows = pl.ds(al(k * 80 + at, 16), 16)
+                    gate_scale = sgu_scales[5 * b + k, pl.ds(0, 1), :]
+                    up_scale = sgu_scales[5 * b + k, pl.ds(1, 1), :]
+                    wshard[rows, 0:HID] = scaled(w0, 4 * k, gate_scale)
+                    wshard[rows, HID : 2 * HID] = (
+                        scaled(w0, 20 + 4 * k, up_scale)
+                        if k < 3
+                        else scaled(w1, 4 * (k - 3), up_scale)
+                    )
                 return 0
 
             lax.fori_loop(0, 5, strip, 0)
-            acc_s[...] += jnp.dot(xperm[...].T, wshard[...], preferred_element_type=F32)
             return 0
 
         lax.fori_loop(0, len(shards_in), one, 0)
+
+    def shared_dot(count):
+        rows = pl.ds(0, BLK * count)
+        acc_s[...] += jnp.dot(xperm[rows, :].T, wshard[rows, :], preferred_element_type=F32)
 
     def activate(acc, target):
         g = acc[:, 0:HID]
@@ -454,19 +495,30 @@
 
         lax.fori_loop(0, len(chunks), one, 0)
 
-    def shared_down(blocks):
+    def shared_chunks(chunks):
         def one(j, _):
-            ee = pick(j, blocks)
-            rows = pl.ds(al(BLK * ee, 16), BLK)
-            turned[...] = dn_all[rows, :].T
-            unpack_down(
-                lambda at: turned[at, :], lambda k: scale_blocks[ee, pl.ds(k, 1), :], wblock
-            )
-            y = jnp.dot(hid_s[...], wblock[...], preferred_element_type=F32)
-            part_s[rows, :] = y.astype(BF16).T
+            cols = pl.ds(al(HID * pick(j, chunks), 128), HID)
+            at = al(128 * pick(j, chunks), 128)
+            for r in range(16):
+                for c in range(5):
+                    turn_in[pl.ds(8 * (5 * r + c), 8), :] = packed[
+                        1, pl.ds(al(at + 8 * r, 8), 8), pl.ds(128 * c, 128)
+                    ]
+            turned[...] = turn_in[...].T
+
+            def strip(q, _):
+                w = turned[pl.ds(al(q * 16, 16), 16), :]
+                for k in range(5):
+                    value = scaled(w, 8 + 4 * k, sdn_scales[pl.ds(k, 1), cols])
+                    wchunk[pl.ds(al(k * 128 + q * 16, 16), 16), :] = value
+                return 0
+
+            lax.fori_loop(0, 8, strip, 0)
+            y = jnp.dot(hid_s[...], wchunk[...], preferred_element_type=F32)
+            part_s[cols, :] = y.astype(BF16).T
             return 0
 
-        lax.fori_loop(0, len(blocks), one, 0)
+        lax.fori_loop(0, len(chunks), one, 0)
 
     local_tok.wait()
     local_ids.wait()
@@ -486,6 +538,7 @@
     local_sgu.wait()
     local_sdn.wait()
     local_gs.wait()
+    pack_own()
 
     def a2a(src, dst, k):
         def one(i, _):
@@ -517,141 +570,125 @@
     unpack_routed(1)
     pl.semaphore_wait(barrier, 18)
 
+    first = BLK * lax.rem(z + 4, NZ) // HID
+
+    def chunks_for(offsets, chunks, total):
+        qs = [lax.rem(first + q, 5) for q in offsets]
+        chunks([5 * other + q for q in qs])
+        for q in qs:
+            cp = total.sibling_copy(HID * q, HID, q)
+            cp.start()
+            sent.append(cp)
+        chunks([5 * core + q for q in qs])
+
+    def chunks_wait(offsets, total):
+        for q in offsets:
+            at = lax.rem(first + q, 5)
+            total.sibling_wait(HID * at, HID, at)
+
+    def hidden_pair(c, r):
+        if c is other:
+            slots.sibling_wait(r)
+            slots.sibling_wait(-r)
+        routed_blocks([block_of(c, r), block_of(c, -r)])
+
     a2a(disp, disp_in, 0)
-    toks.start(True)
-    gate.r0()
-    up.r0()
+    toks.start_whole()
+    low.r0()
+    high.r0()
     unpack_routed(2)
-    toks.start(False)
     unpack_routed(3)
-    down_a.r0()
-    down_b.r0()
     unpack_routed(4)
-    toks.step(1, True)
+    toks.step_whole(1)
     unpack_routed(5)
-    toks.step(1, False)
     unpack_routed(6)
     a2a_wait(disp_in, 0)
     xs_t[own_rows, :] = disp_in[...].T
     slots.start(True)
-    toks.step(2, True)
     unpack_routed(7)
-    toks.step(2, False)
+    toks.step_whole(2)
     unpack_routed(8)
     slots.start(False)
     unpack_routed(9)
-    toks.step(3, True)
     local_ss.wait()
     local_sds.wait()
-    for i in range(16):
-        scale_blocks[i, 0:5, :] = sdn_scales[:, BLK * i : BLK * (i + 1)]
-    down_a.r1()
-    down_b.r1()
-    toks.step(3, False)
-    gate.r1()
-    up.r1()
+    toks.step_whole(3)
+    low.r1()
+    high.r1()
     slots.step(1, True)
-    toks.step(4, True)
     slots.sibling_wait(0)
     routed_blocks([block_of(core, 0), block_of(other, 0)])
+    toks.step_whole(4)
     slots.step(1, False)
-    routed_blocks([block_of(core, 1), block_of(core, -1)])
+    hidden_pair(core, 1)
     for dz in (0, 1, -1, 2, -2, 3, -3, 4):
         toks.sibling_wait(dz)
-    shared_shards(gate.arrived(0))
+    shared_shards(low.arrived(0), 0)
     slots.step(2, True)
-    slots.sibling_wait(1)
-    slots.sibling_wait(-1)
-    routed_blocks([block_of(other, 1), block_of(other, -1)])
-    shared_shards(gate.arrived(1)[0:1])
+    hidden_pair(other, 1)
+    shared_shards(low.arrived(1)[0:1], 1)
     slots.step(2, False)
-    routed_blocks([block_of(core, 2), block_of(core, -2)])
-    shared_shards(gate.arrived(1)[1:2])
+    hidden_pair(core, 2)
+    shared_shards(low.arrived(1)[1:3], 2)
     slots.step(3, True)
-    slots.sibling_wait(2)
-    slots.sibling_wait(-2)
-    routed_blocks([block_of(other, 2), block_of(other, -2)])
-    shared_shards(gate.arrived(1)[2:3])
+    hidden_pair(other, 2)
+    shared_shards(low.arrived(1)[3:4], 4)
     slots.step(3, False)
-    routed_blocks([block_of(core, 3), block_of(core, -3)])
-    shared_shards(gate.arrived(1)[3:4])
-    down_a.r2()
-    down_b.r2()
+    hidden_pair(core, 3)
+    low.r2()
+    high.r2()
     slots.step(4, True)
-    slots.sibling_wait(3)
-    slots.sibling_wait(-3)
+    hidden_pair(other, 3)
     slots.sibling_wait(4)
-    routed_blocks([block_of(c, dz) for c, dz in ((other, 3), (other, -3), (core, 4), (other, 4))])
+    routed_blocks([block_of(core, 4), block_of(other, 4)])
     activate(acc_r, hid_r)
-
     local_ds.wait()
     local_dn.wait()
-    first = BLK * lax.rem(z + 4, NZ) // HID
-
-    def routed_down(offsets):
-        qs = [lax.rem(first + q, 5) for q in offsets]
-        routed_chunks([5 * other + q for q in qs])
-        for q in qs:
-            cp = sum_r.sibling_copy(HID * q, HID, q)
-            cp.start()
-            sent.append(cp)
-        routed_chunks([5 * core + q for q in qs])
-        for q in qs:
-            sum_r.sibling_wait(HID * q, HID, q)
-
-    routed_down((0, 1))
+    chunks_for((0, 1), routed_chunks, sum_r)
+    chunks_wait((0, 1), sum_r)
     sum_r.long_step(0)
-    gate.r2()
-    up.r2()
-    routed_down((4, 2))
+    chunks_for((4, 2), routed_chunks, sum_r)
+    chunks_wait((4, 2), sum_r)
     sum_r.short_step(1)
     sum_r.long_step(1)
-    routed_down((3,))
-    down_a.r3()
-    down_b.r3()
-    shared_shards(gate.arrived(2)[0:2])
+    low.r3()
+    high.r3()
+    shared_dot(5)
+    chunks_for((3,), routed_chunks, sum_r)
+    low.r4()
+    high.r4()
+    chunks_wait((3,), sum_r)
+    shared_shards(low.arrived(2)[0:1], 0)
     sum_r.short_step(2)
-    shared_shards(gate.arrived(2)[2:3])
+    shared_shards(low.arrived(2)[1:3], 1)
     sum_r.long_step(2)
-    shared_shards(gate.arrived(2)[3:6])
-    gate.r3()
-    up.r3()
+    shared_shards(low.arrived(2)[3:6], 3)
     sum_r.short_step(3)
-    shared_shards(gate.arrived(3)[0:1])
+    shared_dot(6)
     sum_r.long_step(3)
-    shared_shards(gate.arrived(3)[1:4])
-    down_a.r4()
-    down_b.r4()
-    gate.r4()
-    up.r4()
-    shared_shards(gate.arrived(4))
+    shared_shards(low.arrived(3), 0)
+    shared_shards(low.arrived(4), 4)
+    shared_dot(5)
     activate(acc_s, hid_s)
-
-    def shared_order(offsets):
-        ds = [lax.rem(z + dz + NZ, NZ) for dz in offsets]
-        shared_down([NZ * other + d for d in ds])
-        for d in ds:
-            cp = sum_s.sibling_copy(BLK * d, BLK, d)
-            cp.start()
-            sent.append(cp)
-        shared_down([NZ * core + d for d in ds])
-        for d in ds:
-            sum_s.sibling_wait(BLK * d, BLK, d)
-
-    shared_order((4,))
+    chunks_for((0, 1), shared_chunks, sum_s)
+    chunks_wait((0, 1), sum_s)
     sum_s.long_step(0)
     back[...] = sum_r.end().astype(BF16).T
     a2a(back, back_in, 1)
-    shared_order((3, -3))
+    chunks_for((4, 2), shared_chunks, sum_s)
+    chunks_wait((4, 2), sum_s)
     sum_s.short_step(1)
     sum_s.long_step(1)
-    shared_order((2, -2))
+    chunks_for((3,), shared_chunks, sum_s)
+    chunks_wait((3,), sum_s)
     sum_s.short_step(2)
     sum_s.long_step(2)
-    shared_order((1, -1))
+    drain(60)
     sum_s.short_step(3)
     sum_s.long_step(3)
-    shared_order((0,))
+    drain(12)
+    a2a_end(disp, 0)
+    a2a_end(back, 1)
     a2a_wait(back_in, 1)
     local_gate.wait()
     routed = lax.dot_general(
@@ -659,10 +696,7 @@
     )
     out[...] = (sum_s.end() + gate_w[...] * routed).astype(BF16)
 
-    a2a_end(disp, 0)
-    a2a_end(back, 1)
-    for cp in sent:
-        cp.wait_send()
+    drain(0)
 
 
 def shards(
@@ -693,19 +727,19 @@
             V((5, 1, D), F32),
             V((50, 2, HID), F32),
             V((5, D), F32),
-            V((16, 8, BLK), F32),
             V((2, 1280, HID), F32),
             V((128, D), F32),
-            V((2, 1280, HID), F32),
-            V((D, 128), F32),
+            V((2, 80, HID), F32),
+            V((BLK, 128), F32),
+            V((2, 1280, HID), I32),
+            V((HID, 128), I32),
             V((D, 2 * HID), BF16),
-            V((BLK, 2 * HID), BF16),
+            V((6 * BLK, 2 * HID), BF16),
             V((HID, HID), BF16),
-            V((HID, BLK), BF16),
-            V((128, BLK), F32),
+            V((128, HID), I32),
             V((D, SLOTS), BF16),
             V((D, TOK), BF16),
-            V((BLK, TOK), BF16),
+            V((6 * BLK, TOK), BF16),
             V((SLOTS, 2 * HID), F32),
             V((TOK, 2 * HID), F32),
             V((SLOTS, HID), BF16),
@@ -723,8 +757,8 @@
             V((SLOTS, BLK), BF16),
             V((SLOTS, BLK), BF16),
             V((SLOTS, BLK), BF16),
-            S((80,)),
-            S((80,)),
+            S((40,)),
+            S((40,)),
             S((64,)),
             S((64,)),
             S((2,)),

time: 93.9 us -> 89.7 us (0.955)
  Pallas kernels: 92.2 us -> 87.5 us
    pallas_call x1, Pallas kernels: 92.2 us -> 87.5 us  [shards(): pl.pallas_call(kernel, out_shape=jax.ShapeDtypeStruct((BLK, TOK), BF16),...]
where the time goes in v4:
time: 89.7 us; the launch traced here: 89.1 us
  Pallas kernels  87.5 us (98%)
  local copies, waits for them, and re-layouts  1.54 us (2%)
    pallas_call x1, Pallas kernels, shards(): pl.pallas_call(kernel, out_shape=jax.ShapeDtypeStruct((BLK, TOK), BF16),...  87.5 us

profile of v4, /device:TPU:1, one launch (start us, length us, event | category | flops | bytes accessed | tf_op | source)
XLA Modules:
  0.0 89.1 jit_solution(10426225113399399087)
XLA Ops:
  0.0 87.5 %shard_map.109 = bf16[400,128]{1,0:T(8,128)(2,1)} custom-call(bf16[400,128]{1,0:T(8,128)(2,1)} %bitcast.19, s32[1,128]{1,0:T(1,128)} %bitcast.20, f32[1,128]{1,0:T(1,128)} %bitcast.21, f32[2,1280,640]{2,1,0:T(8,128)} %bitcast.12, f32[50,2,640]{2,1,0:T(2,128)} %bitcast.15, f32[128,6400]{1,0:T(8,128)} %bitcast.13, f32[5,1,6400]{2,1,0:T(1,128)} %bitcast.18, ...), custom_call_target="tpu_custom_call" | custom-call | tf_op jit(solution)/shard_map/pallas_call | solution.py:718
  87.5 1.5 %copy.13 = bf16[128,400]{0,1:T(8,128)(2,1)} copy(bf16[128,400]{0,1:T(8,128)(2,1)} %bitcast.14) | data formatting | bytes 204800

commit v5 on v4

--- a/solution.py
+++ b/solution.py
@@ -647,38 +647,35 @@
     chunks_for((0, 1), routed_chunks, sum_r)
     chunks_wait((0, 1), sum_r)
     sum_r.long_step(0)
+    shared_dot(5)
     chunks_for((4, 2), routed_chunks, sum_r)
     chunks_wait((4, 2), sum_r)
     sum_r.short_step(1)
     sum_r.long_step(1)
     low.r3()
     high.r3()
-    shared_dot(5)
     chunks_for((3,), routed_chunks, sum_r)
+    chunks_wait((3,), sum_r)
+    shared_shards(low.arrived(2), 0)
+    sum_r.short_step(2)
     low.r4()
     high.r4()
-    chunks_wait((3,), sum_r)
-    shared_shards(low.arrived(2)[0:1], 0)
-    sum_r.short_step(2)
-    shared_shards(low.arrived(2)[1:3], 1)
     sum_r.long_step(2)
-    shared_shards(low.arrived(2)[3:6], 3)
-    sum_r.short_step(3)
     shared_dot(6)
-    sum_r.long_step(3)
-    shared_shards(low.arrived(3), 0)
-    shared_shards(low.arrived(4), 4)
+    shared_shards(low.arrived(3) + low.arrived(4), 0)
     shared_dot(5)
     activate(acc_s, hid_s)
+    sum_r.short_step(3)
+    sum_r.long_step(3)
     chunks_for((0, 1), shared_chunks, sum_s)
     chunks_wait((0, 1), sum_s)
     sum_s.long_step(0)
-    back[...] = sum_r.end().astype(BF16).T
-    a2a(back, back_in, 1)
     chunks_for((4, 2), shared_chunks, sum_s)
     chunks_wait((4, 2), sum_s)
     sum_s.short_step(1)
     sum_s.long_step(1)
+    back[...] = sum_r.end().astype(BF16).T
+    a2a(back, back_in, 1)
     chunks_for((3,), shared_chunks, sum_s)
     chunks_wait((3,), sum_s)
     sum_s.short_step(2)

time: 89.7 us -> 86.4 us (0.963)
  Pallas kernels: 87.5 us -> 84.4 us
    pallas_call x1, Pallas kernels: 87.5 us -> 84.4 us  [shards(): pl.pallas_call(kernel, out_shape=jax.ShapeDtypeStruct((BLK, TOK), BF16),...]
where the time goes in v5:
time: 86.4 us; the launch traced here: 86 us
  Pallas kernels  84.4 us (98%)
  local copies, waits for them, and re-layouts  1.54 us (2%)
    pallas_call x1, Pallas kernels, shards(): pl.pallas_call(kernel, out_shape=jax.ShapeDtypeStruct((BLK, TOK), BF16),...  84.4 us

profile of v5, /device:TPU:1, one launch (start us, length us, event | category | flops | bytes accessed | tf_op | source)
XLA Modules:
  0.0 86.0 jit_solution(11822836157313488393)
XLA Ops:
  0.0 84.4 %shard_map.109 = bf16[400,128]{1,0:T(8,128)(2,1)} custom-call(bf16[400,128]{1,0:T(8,128)(2,1)} %bitcast.19, s32[1,128]{1,0:T(1,128)} %bitcast.20, f32[1,128]{1,0:T(1,128)} %bitcast.21, f32[2,1280,640]{2,1,0:T(8,128)} %bitcast.12, f32[50,2,640]{2,1,0:T(2,128)} %bitcast.15, f32[128,6400]{1,0:T(8,128)} %bitcast.13, f32[5,1,6400]{2,1,0:T(1,128)} %bitcast.18, ...), custom_call_target="tpu_custom_call" | custom-call | tf_op jit(solution)/shard_map/pallas_call | solution.py:715
  84.4 1.5 %copy.13 = bf16[128,400]{0,1:T(8,128)(2,1)} copy(bf16[128,400]{0,1:T(8,128)(2,1)} %bitcast.14) | data formatting | bytes 204800

commit v6 on v5

--- a/solution.py
+++ b/solution.py
@@ -428,7 +428,7 @@
             )
             return 0
 
-        lax.fori_loop(0, len(blocks), one, 0)
+        lax.fori_loop(0, len(blocks), one, 0, unroll=True)
 
     def shared_shards(shards_in, place):
         def one(j, _):
@@ -483,7 +483,7 @@
             digits(words(at), rows_of_scales, store)
             return 0
 
-        lax.fori_loop(0, 8, strip, 0)
+        lax.fori_loop(0, 8, strip, 0, unroll=2)
 
     def routed_chunks(chunks):
         def one(j, _):
@@ -513,7 +513,7 @@
                     wchunk[pl.ds(al(k * 128 + q * 16, 16), 16), :] = value
                 return 0
 
-            lax.fori_loop(0, 8, strip, 0)
+            lax.fori_loop(0, 8, strip, 0, unroll=2)
             y = jnp.dot(hid_s[...], wchunk[...], preferred_element_type=F32)
             part_s[cols, :] = y.astype(BF16).T
             return 0

time: 86.4 us -> 85.4 us (0.988)
  Pallas kernels: 84.4 us -> 83.2 us
    pallas_call x1, Pallas kernels: 84.4 us -> 83.2 us  [shards(): pl.pallas_call(kernel, out_shape=jax.ShapeDtypeStruct((BLK, TOK), BF16),...]
where the time goes in v6:
time: 85.4 us; the launch traced here: 84.8 us
  Pallas kernels  83.2 us (97%)
  local copies, waits for them, and re-layouts  1.54 us (2%)
    pallas_call x1, Pallas kernels, shards(): pl.pallas_call(kernel, out_shape=jax.ShapeDtypeStruct((BLK, TOK), BF16),...  83.2 us

profile of v6, /device:TPU:1, one launch (start us, length us, event | category | flops | bytes accessed | tf_op | source)
XLA Modules:
  0.0 84.8 jit_solution(4912074876364358948)
XLA Ops:
  0.0 83.2 %shard_map.109 = bf16[400,128]{1,0:T(8,128)(2,1)} custom-call(bf16[400,128]{1,0:T(8,128)(2,1)} %bitcast.19, s32[1,128]{1,0:T(1,128)} %bitcast.20, f32[1,128]{1,0:T(1,128)} %bitcast.21, f32[2,1280,640]{2,1,0:T(8,128)} %bitcast.12, f32[50,2,640]{2,1,0:T(2,128)} %bitcast.15, f32[128,6400]{1,0:T(8,128)} %bitcast.13, f32[5,1,6400]{2,1,0:T(1,128)} %bitcast.18, ...), custom_call_target="tpu_custom_call" | custom-call | tf_op jit(solution)/shard_map/pallas_call | solution.py:715
  83.2 1.5 %copy.13 = bf16[128,400]{0,1:T(8,128)(2,1)} copy(bf16[128,400]{0,1:T(8,128)(2,1)} %bitcast.14) | data formatting | bytes 204800
